TPU v7x, 256 devices: a whole 4x4x8 slice. The times are simulated.
256 devices in a mesh: seq: 32 (over x, y, core), blk: 8 (over z).
Axes of the slice: x: 4, y: 4, z: 8, core: 2. Of those that a mesh axis runs over, the one named last changes fastest.
Arguments:
- alphas: float32 [2, 2048, 32768], P(None, 'seq', 'blk'), may hold values from 0.05 to 1
- betas: float32 [2, 2048, 65536], P(None, 'seq', 'blk'), may hold values from 0.05 to 1
- token_ids: int32 [2, 2048], P(None, 'seq'), may hold values from 0 to 31
- emission: float32 [32, 65536], P(None, 'blk'), may hold values from 0.05 to 1
- left_blocks: float32 [64, 128, 512], P('blk'), may hold values from 0.000390625 to 0.00390625
- right_blocks: float32 [128, 64, 512], P('blk', 'seq'), may hold values from 0.003125 to 0.03125
Outputs:
- left_grad: float32 [64, 128, 512], P('blk', 'seq')
- right_grad: float32 [128, 64, 512], P('blk', 'seq')
All inputs are finite; a program needn't handle non-finite values.
Results may differ from a plain program's by a relative error of at most 0.0001.
Values sent between devices are 32-bit elements; how exact they have to be, the bound alone decides.
No kernel may reach another device: no remote copies, remote signals or barrier semaphores. Data moves between devices by JAX's collectives and lax.ppermute only.
A program may use at most 128 MiB of HBM per device.

v0:
```python
import functools

import jax
import jax.numpy as jnp
from jax import lax
from jax.experimental import pallas as pl
from jax.experimental.pallas import tpu as pltpu
from jax.sharding import Mesh, PartitionSpec as P

F32 = jnp.float32
BF16 = jnp.bfloat16
NT = (((1,), (1,)), ((), ()))
NN = (((1,), (0,)), ((), ()))
TN = (((0,), (0,)), ((), ()))
LANES = 128
MIB = 1024 * 1024
ANYWHERE = pl.BlockSpec(memory_space=pl.ANY)
WHOLE = pl.BlockSpec(memory_space=pltpu.VMEM)
SCALARS = pl.BlockSpec(memory_space=pltpu.SMEM)


def split(value):
    high = value.astype(BF16)
    low = (value - high.astype(F32)).astype(BF16)
    return high, low


def start(source, target, sem):
    copy = pltpu.make_async_copy(source, target, sem)
    copy.start()
    return copy


def dot3(a, b, dims):
    (ah, al), (bh, bl) = split(a), split(b)
    part = functools.partial(lax.dot_general, dimension_numbers=dims, preferred_element_type=F32)
    rows = a.shape[0]
    both = part(jnp.concatenate([ah, al], axis=0), bh)
    return both[:rows] + (part(ah, bl) + both[rows:])


def signal_kernel(tok_ref, emission_ref, betas_ref, g_ref, table_ref, held_ref, in_sem, out_sem):
    uniq, states = emission_ref.shape
    rows = betas_ref.shape[0]
    pieces = out_sem.shape[0]
    width = states // pieces
    waits = []
    for piece in range(pieces):
        columns = pl.ds(piece * width, width)
        waits.append(
            (
                start(emission_ref.at[:, columns], table_ref.at[:, columns], in_sem.at[0, piece]),
                start(betas_ref.at[:, columns], held_ref.at[:, columns], in_sem.at[1, piece]),
            )
        )
    tokens = jnp.concatenate([tok_ref[t : t + 1, :] for t in range(tok_ref.shape[0])], axis=1)
    pick = (lax.broadcasted_iota(jnp.int32, (uniq, rows), 0) == tokens).astype(F32).astype(BF16)
    pick = jnp.concatenate([pick, pick, pick], axis=0)
    outs = []
    for piece in range(pieces):
        columns = pl.ds(piece * width, width)
        for copy in waits[piece]:
            copy.wait()
        table = table_ref[:, columns]
        high, rest = split(table)
        middle, low = split(table - high.astype(F32))
        picked = lax.dot_general(
            pick, jnp.concatenate([high, middle, low], axis=0), TN, preferred_element_type=F32
        )
        held_ref[:, columns] = picked * held_ref[:, columns]
        outs.append(start(held_ref.at[:, columns], g_ref.at[:, columns], out_sem.at[piece]))
    for copy in outs:
        copy.wait()


def signal(tokens, emission, betas):
    pieces = 8
    return pl.pallas_call(
        signal_kernel,
        in_specs=[pl.BlockSpec(memory_space=pltpu.VMEM), ANYWHERE, ANYWHERE],
        out_specs=ANYWHERE,
        out_shape=pltpu.HBM(betas.shape, F32),
        scratch_shapes=[
            pltpu.VMEM(emission.shape, F32),
            pltpu.VMEM(betas.shape, F32),
            pltpu.SemaphoreType.DMA((2, pieces)),
            pltpu.SemaphoreType.DMA((pieces,)),
        ],
        compiler_params=pltpu.CompilerParams(vmem_limit_bytes=16 * MIB),
        name="signal",
    )(tokens, emission, betas)


def mixed_kernel(rows_hbm, left_hbm, u_ref, rows_ref, left_ref, sem):
    blocks, _, width = left_ref.shape
    waits = []
    for i in range(blocks):
        columns = pl.ds(i * width, width)
        waits.append(
            (
                start(rows_hbm.at[:, columns], rows_ref.at[i], sem.at[0, i]),
                start(left_hbm.at[i], left_ref.at[i], sem.at[1, i]),
            )
        )
    zs, height, _ = u_ref.shape
    part = height // blocks
    for i in range(blocks):
        for copy in waits[i]:
            copy.wait()
        u = dot3(left_ref[i], rows_ref[i], NT)
        for z in range(zs):
            u_ref[z, i * part : (i + 1) * part, :] = u[z * part : (z + 1) * part]


def mixed(alphas, left, zs):
    rows = alphas.shape[0]
    blocks, window, width = left.shape
    return pl.pallas_call(
        mixed_kernel,
        in_specs=[ANYWHERE, ANYWHERE],
        out_specs=WHOLE,
        out_shape=jax.ShapeDtypeStruct((zs, blocks * window // zs, rows), F32),
        scratch_shapes=[
            pltpu.VMEM((blocks, rows, width), F32),
            pltpu.VMEM(left.shape, F32),
            pltpu.SemaphoreType.DMA((2, blocks)),
        ],
        compiler_params=pltpu.CompilerParams(vmem_limit_bytes=8 * MIB),
        name="mixed",
    )(alphas, left)


def place_of(k):
    return (k // 4 % 2) * 8 + k // 8 * 4 + k % 4


def back_kernel(kcount, ways, place_ref, *refs):
    slots = len(ways[0])
    rights, refs = (refs[:slots], refs[slots : 2 * slots]), refs[2 * slots :]
    signal_ref, u_ref, h_ref, send_ref, g_ref, right_ref, held_ref, sem = refs
    lanes = u_ref.shape[1]
    steps = sem.shape[0]
    share = g_ref.shape[1] // steps
    waits = []
    for step in range(steps):
        columns = pl.ds(step * share, share)
        waits.append(start(signal_ref.at[:, columns], g_ref.at[:, columns], sem.at[step]))
    nx, ny = slots, len(ways[1])
    chips = nx * ny
    width = g_ref.shape[1] // kcount
    pieces = width // lanes
    krows = 4 * kcount
    rrows = right_ref.shape[1] // chips
    core = place_ref[2]
    for side in range(2):
        owner = core if side == 0 else 1 - core
        for a, dx in enumerate(ways[0]):
            for b, dy in enumerate(ways[1]):
                x = lax.rem(place_ref[0] + (nx - dx), nx)
                y = lax.rem(place_ref[1] + (ny - dy), ny)
                chip = pl.multiple_of((x * ny + y) * rrows, rrows)
                right_ref[owner, pl.ds(chip, rrows), :] = rights[side][a][b * rrows : (b + 1) * rrows, :]

    part = 2 * kcount
    theirs = pl.multiple_of((1 - core) * part, part)
    for chip in range(chips):
        send_ref[chip * part : (chip + 1) * part, :] = u_ref[pl.ds(chip * 2 * part + theirs, part), :]

    total = jnp.zeros((8, lanes), F32)
    for k in range(kcount):
        if k * steps % kcount == 0:
            waits[k * steps // kcount].wait()
        r = jnp.concatenate(
            [
                jnp.concatenate(
                    [
                        right_ref[c, pl.ds(k * 2 * pieces + 2 * piece + e, chips, stride=rrows), :]
                        for piece in range(pieces)
                    ],
                    axis=1,
                )
                for c in range(2)
                for e in range(2)
            ],
            axis=0,
        )
        h = dot3(r, g_ref[:, k * width : (k + 1) * width], NT)
        for i in range(4):
            mine = h[i * chips : (i + 1) * chips, :]
            held_ref[pl.ds(i * kcount + place_of(k), chips, stride=krows), :] = mine
            both = u_ref[pl.ds(i * kcount + k, chips, stride=krows), :] * mine
            for top in range(0, chips, 8):
                total = total + both[top : top + 8, :]
    zs, height, _ = h_ref.shape
    body = height - 8
    total = jnp.broadcast_to(jnp.sum(total, axis=0, keepdims=True), total.shape)
    for z in range(zs):
        h_ref[z, 0:body, :] = held_ref[z * body : (z + 1) * body, :]
        h_ref[z, body:height, :] = total


def back(place, ways, rights, others, own, u, zs, kcount):
    rows, states = own.shape
    body = u.shape[0] // zs
    right = (2, rights[0].shape[0] * len(rights), rights[0].shape[1])
    return pl.pallas_call(
        functools.partial(back_kernel, kcount, ways),
        in_specs=[SCALARS, *[WHOLE for _ in (*rights, *others)], ANYWHERE, WHOLE],
        out_specs=(WHOLE, WHOLE),
        out_shape=(
            jax.ShapeDtypeStruct((zs, body + 8, rows), F32),
            jax.ShapeDtypeStruct((u.shape[0] // 2, rows), F32),
        ),
        scratch_shapes=[
            pltpu.VMEM((rows, states), F32),
            pltpu.VMEM(right, F32),
            pltpu.VMEM(u.shape, F32),
            pltpu.SemaphoreType.DMA((4,)),
        ],
        compiler_params=pltpu.CompilerParams(vmem_limit_bytes=16 * MIB),
        name="back",
    )(place, *rights, *others, own, u)


def pick_h_kernel(place_ref, h_ref, send_ref):
    zs, height, _ = h_ref.shape
    first = pl.multiple_of((1 - place_ref[2]) * 8, 8)
    total = h_ref[0, height - 8 : height, :]
    for z in range(1, zs):
        total = total + h_ref[z, height - 8 : height, :]
    bands = (height - 8) // 16
    for z in range(zs):
        for band in range(bands):
            send_ref[(z * bands + band) * 8 : (z * bands + band + 1) * 8, :] = h_ref[z, pl.ds(band * 16 + first, 8), :]
    send_ref[zs * bands * 8 :, :] = total


def pick_h(place, h):
    zs, height, lanes = h.shape
    return pl.pallas_call(
        pick_h_kernel,
        in_specs=[SCALARS, WHOLE],
        out_specs=WHOLE,
        out_shape=jax.ShapeDtypeStruct((zs * (height - 8) // 2 + 8, lanes), F32),
        compiler_params=pltpu.CompilerParams(vmem_limit_bytes=4 * MIB),
        name="pick_h",
    )(place, h)


def gradients_kernel(kcount, scale, place_ref, h_ref, sent_ref, got_ref, u_ref, uo_ref, *refs):
    rows_refs, g_refs, (out_ref, rows_ref, g_ref, rows_sem, g_sem) = refs[:2], refs[2:4], refs[4:]
    blocks, both, width = rows_ref.shape
    lanes = both // 2
    rows_waits, g_waits = [], []
    for i in range(blocks):
        columns = pl.ds(i * width, width)
        rows_waits.append(
            [start(rows_refs[n].at[:, columns], rows_ref.at[i, pl.ds(n * lanes, lanes)], rows_sem.at[n, i]) for n in range(2)]
        )
    steps = g_sem.shape[1]
    share = g_ref.shape[1] // steps
    for step in range(steps):
        columns = pl.ds(step * share, share)
        g_waits.append(
            [start(g_refs[n].at[:, columns], g_ref.at[pl.ds(n * lanes, lanes), columns], g_sem.at[n, step]) for n in range(2)]
        )
    core = place_ref[2]
    chips, out_rows, _ = out_ref.shape
    pieces = width // lanes
    zs = h_ref.shape[0]
    last = sent_ref.shape[0] - 8
    weights = [scale / sent_ref[last : last + 1, :], scale / got_ref[last : last + 1, :]]

    keep = pl.multiple_of(core * 8, 8)
    for i in range(blocks):
        own = jnp.concatenate([h_ref[z, pl.ds(i * 16 + keep, 8), :] for z in range(zs)], axis=0)
        other = jnp.concatenate([got_ref[(z * blocks + i) * 8 : (z * blocks + i + 1) * 8, :] for z in range(zs)], axis=0)
        h = jnp.concatenate([own * weights[0], other * weights[1]], axis=1)
        for copy in rows_waits[i]:
            copy.wait()
        grad = dot3(h, rows_ref[i], NN)
        depth = grad.shape[0] // chips
        for chip in range(chips):
            for piece in range(pieces):
                first = (i * pieces + piece) * depth
                out_ref[chip, first : first + depth, :] = grad[
                    chip * depth : (chip + 1) * depth, piece * lanes : (piece + 1) * lanes
                ]

    middle = out_rows // 2
    flat_ref = out_ref.reshape(chips * out_rows, lanes)
    g_width = g_ref.shape[1] // kcount
    g_pieces = g_width // lanes
    for k in range(kcount):
        if k * steps % kcount == 0:
            for copy in g_waits[k * steps // kcount]:
                copy.wait()
        u = jnp.concatenate(
            [
                jnp.concatenate(
                    [
                        u_ref[pl.ds((2 * core + e) * kcount + k, chips, stride=4 * kcount), :] * weights[0],
                        uo_ref[pl.ds(e * kcount + k, chips, stride=2 * kcount), :] * weights[1],
                    ],
                    axis=1,
                )
                for e in range(2)
            ],
            axis=0,
        )
        grad = dot3(u, g_ref[:, k * g_width : (k + 1) * g_width], NN)
        for e in range(2):
            for piece in range(g_pieces):
                place = pl.ds(middle + (k * g_pieces + piece) * 2 + e, chips, stride=out_rows)
                flat_ref[place, :] = grad[e * chips : (e + 1) * chips, piece * lanes : (piece + 1) * lanes]


def gradients(place, h, sent, got, u, u_other, alphas, g, chips, kcount, blocks, scale):
    rows, states_in = alphas[0].shape
    states = g[0].shape[1]
    out_rows = (blocks // 2 * (states_in // blocks) * kcount * h.shape[0] + 2 * states * chips) // LANES // chips
    steps = 4
    return pl.pallas_call(
        functools.partial(gradients_kernel, kcount, scale),
        in_specs=[SCALARS] + [WHOLE] * 5 + [ANYWHERE] * 4,
        out_specs=WHOLE,
        out_shape=jax.ShapeDtypeStruct((chips, out_rows, LANES), F32),
        scratch_shapes=[
            pltpu.VMEM((blocks, 2 * rows, states_in // blocks), F32),
            pltpu.VMEM((2 * rows, states), F32),
            pltpu.SemaphoreType.DMA((2, blocks)),
            pltpu.SemaphoreType.DMA((2, steps)),
        ],
        compiler_params=pltpu.CompilerParams(vmem_limit_bytes=16 * MIB),
        name="gradients",
    )(place, h, sent, got, u, u_other, *alphas, *g)


def turn(value, axis, distance):
    if distance == 0:
        return value
    n = lax.axis_size(axis)
    return lax.ppermute(value, axis, [(i, (i + distance) % n) for i in range(n)])


def local(alphas, betas, token_ids, emission, left_blocks, right_blocks):
    steps, seq_dev, states_in = alphas.shape
    states_out = betas.shape[2]
    rows = steps * seq_dev
    blocks, window, width = left_blocks.shape
    kcount, rows_right, nblocks = right_blocks.shape
    zs = lax.axis_size("z")
    chips = lax.axis_size("x") * lax.axis_size("y")
    pieces = nblocks // LANES
    scale = window * nblocks / (2.0 * seq_dev * chips * 2)
    swap = functools.partial(lax.ppermute, axis_name="c", perm=[(0, 1), (1, 0)])
    in_hbm = functools.partial(pltpu.with_memory_space_constraint, memory_space=pltpu.HBM)
    place = jnp.stack([lax.axis_index(name) for name in ("x", "y", "c")]).astype(jnp.int32)
    alphas = alphas.reshape(rows, states_in)
    betas = in_hbm(betas.reshape(rows, states_out))

    right_rows = right_blocks.reshape(kcount, rows_right, pieces, LANES).transpose(0, 2, 1, 3)
    right_rows = right_rows.reshape(kcount * pieces * rows_right, LANES)
    ways = tuple((0, 1, n - 1) + tuple(range(2, n - 1)) for n in (lax.axis_size("x"), lax.axis_size("y")))
    right_y = jnp.concatenate([turn(right_rows, "y", d) for d in ways[1]], axis=0)

    u = mixed(in_hbm(alphas), in_hbm(left_blocks), zs)
    u, right_y = lax.optimization_barrier((u, right_y))
    u = lax.all_to_all(u, "z", split_axis=0, concat_axis=0, tiled=True).reshape(-1, rows)
    rights = [turn(right_y, "x", d) for d in ways[0]]
    g_own = signal(token_ids, in_hbm(emission), betas)
    rights[1], g_own = lax.optimization_barrier((rights[1], g_own))
    others = [swap(part) for part in rights]

    h, u_sent = back(place, ways, rights, others, in_hbm(g_own), u, zs, kcount)
    h, g_later = lax.optimization_barrier((h, g_own))
    h = lax.all_to_all(h, "z", split_axis=0, concat_axis=0, tiled=True)
    sent = pick_h(place, h)
    got = swap(sent)

    u_other = swap(u_sent)
    two_alphas, two_g = (in_hbm(alphas), swap(alphas)), (in_hbm(g_later), swap(g_later))
    part = gradients(place, h, sent, got, u, u_other, two_alphas, two_g, chips, kcount, blocks, scale)
    parts = lax.all_to_all(part, ("x", "y"), split_axis=0, concat_axis=0, tiled=True)
    total = jnp.sum(parts, axis=0)
    middle = total.shape[0] // 2
    left_grad = total[:middle].reshape(blocks, pieces, -1, LANES).transpose(0, 2, 1, 3).reshape(blocks, -1, width)
    right_grad = total[middle:].reshape(kcount, pieces, rows_right, LANES).transpose(0, 2, 1, 3)
    return left_grad, right_grad.reshape(kcount, rows_right, nblocks)


def solution(mesh):
    seq, blk = mesh.shape["seq"], mesh.shape["blk"]
    side = round((seq // 2) ** 0.5)
    fine = Mesh(mesh.devices.reshape(side, seq // 2 // side, 2, blk), ("x", "y", "c", "z"))
    s = ("x", "y", "c")
    placed = (
        P(None, s, "z"),
        P(None, s, "z"),
        P(None, s),
        P(None, "z"),
        P("z", None, None),
        P("z", s, None),
    )
    return jax.shard_map(
        local,
        mesh=fine,
        in_specs=placed,
        out_specs=(P("z", s, None), P("z", s, None)),
        check_vma=False,
    )
```

profile of v0, /device:TPU:2, one launch (start us, length us, event | category | flops | bytes accessed | tf_op | source)
XLA Modules:
  0.0 109.1 jit_solution(10525608719076939894)
XLA Ops:
  0.6 3.3 %collective-permute-start.2 = (f32[128,128]{1,0:T(8,128)}, f32[128,128]{1,0:T(8,128)S(1)}, u32[]{:S(2)}, u32[]{:S(2)}) collective-permute-start(f32[128,128]{1,0:T(8,128)} %bitcast.29), channel_id=1, source_target_pairs={{0,32},{16,48},{32,0},{48,16},{1,33},{17,49},{33,1},{49,17},{2,34}... | collective-permute-start | bytes 196616 | tf_op jit(solution)/shard_map/ppermute | solution.py:343
  3.9 1.1 collective-permute-start.1
  5.0 1.0 collective-permute-start
  5.9 0.0 copy-start.3
  5.9 0.0 copy-start
  5.9 4.8 %mixed.1 = f32[8,128,128]{2,1,0:T(8,128)} custom-call(f32[128,4096]{1,0:T(8,128)} %bitcast.23, f32[8,128,512]{2,1,0:T(8,128)} %left_hbm.1), custom_call_target="tpu_custom_call" | custom-call | tf_op jit(solution)/shard_map/mixed/pallas_call | solution.py:118
  10.8 0.0 collective-permute-done.2
  10.8 0.0 collective-permute-done.1
  10.8 0.0 collective-permute-done
  10.8 0.0 copy-done.3
  10.8 8.5 %all-to-all-start = ((f32[8,128,128]{2,1,0:T(8,128)}), f32[8,128,128]{2,1,0:T(8,128)S(1)}, u32[]{:S(2)}, u32[]{:S(2)}) async-start(f32[8,128,128]{2,1,0:T(8,128)} %mixed.1), calls=%async_computation | async-start | bytes 1048576 | tf_op jit(solution)/shard_map/all_to_all | solution.py:369
  19.3 1.5 %collective-permute-start.3 = (f32[512,128]{1,0:T(8,128)S(1)}, f32[512,128]{1,0:T(8,128)S(1)}, u32[]{:S(2)}, u32[]{:S(2)}) collective-permute-start(f32[512,128]{1,0:T(8,128)S(1)} %pad_maximum_fusion.refs_0_), channel_id=1, source_target_pairs={{0,64},{64,128},{128,192},{192,0},{1,65},{65,129},{129,193},{193,1... | collective-permute-start | bytes 786440 | tf_op jit(solution)/shard_map/ppermute | solution.py:343
  20.8 1.1 %collective-permute-start.5 = (f32[512,128]{1,0:T(8,128)S(1)}, f32[512,128]{1,0:T(8,128)S(1)}, u32[]{:S(2)}, u32[]{:S(2)}) collective-permute-start(f32[512,128]{1,0:T(8,128)S(1)} %pad_maximum_fusion.refs_0_), channel_id=1, source_target_pairs={{0,128},{64,192},{128,0},{192,64},{1,129},{65,193},{129,1},{193,65... | collective-permute-start | bytes 786440 | tf_op jit(solution)/shard_map/ppermute | solution.py:343
  21.9 2.2 %collective-permute-start.4 = (f32[512,128]{1,0:T(8,128)S(1)}, f32[512,128]{1,0:T(8,128)S(1)}, u32[]{:S(2)}, u32[]{:S(2)}) collective-permute-start(f32[512,128]{1,0:T(8,128)S(1)} %pad_maximum_fusion.refs_0_), channel_id=1, source_target_pairs={{0,192},{64,0},{128,64},{192,128},{1,193},{65,1},{129,65},{193,129... | collective-permute-start | bytes 786440 | tf_op jit(solution)/shard_map/ppermute | solution.py:343
  24.1 0.0 copy-done
  24.1 4.3 %signal.1.refs_8_.refs_2_ = f32[128,8192]{1,0:T(8,128)} custom-call(s32[2,64]{1,0:T(2,128)S(1)} %copy-done, f32[32,8192]{1,0:T(8,128)} %emission_ref.1, f32[128,8192]{1,0:T(8,128)} %bitcast.26), custom_call_target="tpu_custom_call" | custom-call | tf_op jit(solution)/shard_map/signal/pallas_call | solution.py:78
  28.4 0.1 collective-permute-start.6
  28.5 0.1 collective-permute-done.3.refs_1_
  28.6 3.0 %collective-permute-done.5.refs_3_ = f32[512,128]{1,0:T(8,128)S(1)} collective-permute-done((f32[512,128]{1,0:T(8,128)S(1)}, f32[512,128]{1,0:T(8,128)S(1)}, u32[]{:S(2)}, u32[]{:S(2)}) %collective-permute-start.5) | collective-permute-done | bytes 262176 | tf_op jit(solution)/shard_map/ppermute | solution.py:343
  31.6 0.0 collective-permute-start.9
  31.6 2.3 %collective-permute-done.4.refs_2_ = f32[512,128]{1,0:T(8,128)S(1)} collective-permute-done((f32[512,128]{1,0:T(8,128)S(1)}, f32[512,128]{1,0:T(8,128)S(1)}, u32[]{:S(2)}, u32[]{:S(2)}) %collective-permute-start.4) | collective-permute-done | bytes 262176 | tf_op jit(solution)/shard_map/ppermute | solution.py:343
  33.9 0.0 collective-permute-start.8
  33.9 0.5 collective-permute-start.7
  34.4 0.1 pad_add_fusion.place_ref
  34.5 0.0 collective-permute-done.6.refs_4_
  34.5 0.0 collective-permute-done.9.refs_7_
  34.5 0.9 collective-permute-done.8.refs_6_
  35.4 0.4 collective-permute-done.7.refs_5_
  35.8 0.2 all-to-all-done
  36.0 0.0 copy-start.1
  36.0 0.0 copy-start.2
  36.0 5.2 %back.1 = (f32[8,136,128]{2,1,0:T(8,128)S(1)}, f32[512,128]{1,0:T(8,128)S(1)}) custom-call(s32[3]{0:T(128)S(1)} %pad_add_fusion.place_ref, f32[512,128]{1,0:T(8,128)S(1)} %pad_maximum_fusion.refs_0_, f32[512,128]{1,0:T(8,128)S(1)} %collective-permute-done.3.refs_1_, f32[512,128]{1,0:T(8,128)S(1)} %collective-permute-done.4.refs_2_, ...), custom_call_target="tpu_custom_call" | custom-call | tf_op jit(solution)/shard_map/back/pallas_call | solution.py:206
  41.2 0.0 copy-done.1
  41.2 0.3 collective-permute-start.13
  41.5 0.0 copy-done.2
  41.5 0.5 collective-permute-start.12
  42.0 25.1 %all_to_all.15.h_ref = f32[8,136,128]{2,1,0:T(8,128)S(1)} all-to-all(f32[8,136,128]{2,1,0:T(8,128)S(1)} %get-tuple-element.15), channel_id=1, replica_groups=mesh['x'=4,'y'=4,'c'=2,'z'=8] {'z'}, dimensions={0} | all-to-all | bytes 1114112 | tf_op jit(solution)/shard_map/all_to_all | solution.py:377
  67.0 0.6 pick_h.1.sent_ref
  67.6 0.1 collective-permute-start.10
  67.7 0.5 collective-permute-start.11
  68.2 1.4 %collective-permute-done.11.uo_ref = f32[512,128]{1,0:T(8,128)S(1)} collective-permute-done((f32[512,128]{1,0:T(8,128)S(1)}, f32[512,128]{1,0:T(8,128)S(1)}, u32[]{:S(2)}, u32[]{:S(2)}) %collective-permute-start.11) | collective-permute-done | bytes 262176 | tf_op jit(solution)/shard_map/ppermute | solution.py:381
  69.6 0.0 collective-permute-done.12.refs_1_
  69.6 0.0 collective-permute-done.10.got_ref
  69.6 0.0 collective-permute-done.13.refs_3_
  69.6 6.2 %gradients.1 = f32[16,256,128]{2,1,0:T(8,128)S(1)} custom-call(s32[3]{0:T(128)S(1)} %pad_add_fusion.place_ref, f32[8,136,128]{2,1,0:T(8,128)S(1)} %all_to_all.15.h_ref, f32[520,128]{1,0:T(8,128)S(1)} %pick_h.1.sent_ref, f32[520,128]{1,0:T(8,128)S(1)} %collective-permute-done.10.got_ref, f32[1024,128]{1,0:T(8,128)S(1)} %bitcast.22, ...), custom_call_target="tpu_custom_call" | custom-call | tf_op jit(solution)/shard_map/gradients/pallas_call | solution.py:323
  75.8 32.5 %all_to_all.16 = f32[16,256,128]{2,1,0:T(8,128)S(1)} all-to-all(f32[16,256,128]{2,1,0:T(8,128)S(1)} %gradients.1), channel_id=1, replica_groups=mesh['x'=4,'y'=4,'c'=2,'z'=8] {'x','y'}, dimensions={0} | all-to-all | bytes 4194304 | tf_op jit(solution)/shard_map/all_to_all | solution.py:384
  108.3 0.1 reduce_sum.9
  108.4 0.7 fusion
  (1 shorter events, 0.0 us)
Async XLA Ops:
  0.6 10.1 %collective-permute-start.2 = (f32[128,128]{1,0:T(8,128)}, f32[128,128]{1,0:T(8,128)S(1)}, u32[]{:S(2)}, u32[]{:S(2)}) collective-permute-start(f32[128,128]{1,0:T(8,128)} %bitcast.29), channel_id=1, source_target_pairs={{0,32},{16,48},{32,0},{48,16},{1,33},{17,49},{33,1},{49,17},{2,34}... | collective-permute-start | bytes 196616 | tf_op jit(solution)/shard_map/ppermute | solution.py:343
  3.9 6.9 %collective-permute-start.1 = (f32[128,128]{1,0:T(8,128)}, f32[128,128]{1,0:T(8,128)S(1)}, u32[]{:S(2)}, u32[]{:S(2)}) collective-permute-start(f32[128,128]{1,0:T(8,128)} %bitcast.30), channel_id=1, source_target_pairs={{0,48},{16,0},{32,16},{48,32},{1,49},{17,1},{33,17},{49,33},{2,50}... | collective-permute-start | bytes 196616 | tf_op jit(solution)/shard_map/ppermute | solution.py:343
  5.0 5.8 %collective-permute-start = (f32[128,128]{1,0:T(8,128)}, f32[128,128]{1,0:T(8,128)S(1)}, u32[]{:S(2)}, u32[]{:S(2)}) collective-permute-start(f32[128,128]{1,0:T(8,128)} %bitcast.31), channel_id=1, source_target_pairs={{0,16},{16,32},{32,48},{48,0},{1,17},{17,33},{33,49},{49,1},{2,18}... | collective-permute-start | bytes 196616 | tf_op jit(solution)/shard_map/ppermute | solution.py:343
  5.9 4.9 %copy-start.3 = (f32[16,2,512]{2,1,0:T(2,128)S(1)}, f32[16,2,512]{2,1,0:T(2,128)}, u32[]{:S(2)}) copy-start(f32[16,2,512]{2,1,0:T(2,128)} %param.11) | copy-start | bytes 196612
  5.9 18.1 %copy-start = (s32[2,64]{1,0:T(2,128)S(1)}, s32[2,64]{1,0:T(2,128)}, u32[]{:S(2)}) copy-start(s32[2,64]{1,0:T(2,128)} %tok_ref.1) | copy-start | bytes 1540
  10.8 25.1 %all-to-all-start = ((f32[8,128,128]{2,1,0:T(8,128)}), f32[8,128,128]{2,1,0:T(8,128)S(1)}, u32[]{:S(2)}, u32[]{:S(2)}) async-start(f32[8,128,128]{2,1,0:T(8,128)} %mixed.1), calls=%async_computation | async-start | bytes 1048576 | tf_op jit(solution)/shard_map/all_to_all | solution.py:369
  19.3 9.2 %collective-permute-start.3 = (f32[512,128]{1,0:T(8,128)S(1)}, f32[512,128]{1,0:T(8,128)S(1)}, u32[]{:S(2)}, u32[]{:S(2)}) collective-permute-start(f32[512,128]{1,0:T(8,128)S(1)} %pad_maximum_fusion.refs_0_), channel_id=1, source_target_pairs={{0,64},{64,128},{128,192},{192,0},{1,65},{65,129},{129,193},{193,1... | collective-permute-start | bytes 786440 | tf_op jit(solution)/shard_map/ppermute | solution.py:343
  20.8 10.8 %collective-permute-start.5 = (f32[512,128]{1,0:T(8,128)S(1)}, f32[512,128]{1,0:T(8,128)S(1)}, u32[]{:S(2)}, u32[]{:S(2)}) collective-permute-start(f32[512,128]{1,0:T(8,128)S(1)} %pad_maximum_fusion.refs_0_), channel_id=1, source_target_pairs={{0,128},{64,192},{128,0},{192,64},{1,129},{65,193},{129,1},{193,65... | collective-permute-start | bytes 786440 | tf_op jit(solution)/shard_map/ppermute | solution.py:343
  21.9 12.0 %collective-permute-start.4 = (f32[512,128]{1,0:T(8,128)S(1)}, f32[512,128]{1,0:T(8,128)S(1)}, u32[]{:S(2)}, u32[]{:S(2)}) collective-permute-start(f32[512,128]{1,0:T(8,128)S(1)} %pad_maximum_fusion.refs_0_), channel_id=1, source_target_pairs={{0,192},{64,0},{128,64},{192,128},{1,193},{65,1},{129,65},{193,129... | collective-permute-start | bytes 786440 | tf_op jit(solution)/shard_map/ppermute | solution.py:343
  28.4 6.1 %collective-permute-start.6 = (f32[512,128]{1,0:T(8,128)S(1)}, f32[512,128]{1,0:T(8,128)S(1)}, u32[]{:S(2)}, u32[]{:S(2)}) collective-permute-start(f32[512,128]{1,0:T(8,128)S(1)} %pad_maximum_fusion.refs_0_), channel_id=1, source_target_pairs={{0,8},{8,0},{1,9},{9,1},{2,10},{10,2},{3,11},{11,3},{4,12},{12,4},... | collective-permute-start | bytes 786440 | tf_op jit(solution)/shard_map/ppermute | solution.py:373
  31.6 2.9 %collective-permute-start.9 = (f32[512,128]{1,0:T(8,128)S(1)}, f32[512,128]{1,0:T(8,128)S(1)}, u32[]{:S(2)}, u32[]{:S(2)}) collective-permute-start(f32[512,128]{1,0:T(8,128)S(1)} %collective-permute-done.5.refs_3_), channel_id=1, source_target_pairs={{0,8},{8,0},{1,9},{9,1},{2,10},{10,2},{3,11},{11,3},{4,12},{12,4},... | collective-permute-start | bytes 786440 | tf_op jit(solution)/shard_map/ppermute | solution.py:373
  33.9 1.5 %collective-permute-start.8 = (f32[512,128]{1,0:T(8,128)S(1)}, f32[512,128]{1,0:T(8,128)S(1)}, u32[]{:S(2)}, u32[]{:S(2)}) collective-permute-start(f32[512,128]{1,0:T(8,128)S(1)} %collective-permute-done.4.refs_2_), channel_id=1, source_target_pairs={{0,8},{8,0},{1,9},{9,1},{2,10},{10,2},{3,11},{11,3},{4,12},{12,4},... | collective-permute-start | bytes 786440 | tf_op jit(solution)/shard_map/ppermute | solution.py:373
  33.9 1.9 %collective-permute-start.7 = (f32[512,128]{1,0:T(8,128)S(1)}, f32[512,128]{1,0:T(8,128)S(1)}, u32[]{:S(2)}, u32[]{:S(2)}) collective-permute-start(f32[512,128]{1,0:T(8,128)S(1)} %collective-permute-done.3.refs_1_), channel_id=1, source_target_pairs={{0,8},{8,0},{1,9},{9,1},{2,10},{10,2},{3,11},{11,3},{4,12},{12,4},... | collective-permute-start | bytes 786440 | tf_op jit(solution)/shard_map/ppermute | solution.py:373
  36.0 5.2 %copy-start.1 = (f32[128,8192]{1,0:T(8,128)S(1)}, f32[128,8192]{1,0:T(8,128)}, u32[]{:S(2)}) copy-start(f32[128,8192]{1,0:T(8,128)} %signal.1.refs_8_.refs_2_) | copy-start | bytes 12582916
  36.0 5.5 %copy-start.2 = (f32[2,64,4096]{2,1,0:T(8,128)S(1)}, f32[2,64,4096]{2,1,0:T(8,128)}, u32[]{:S(2)}) copy-start(f32[2,64,4096]{2,1,0:T(8,128)} %param.6) | copy-start | bytes 6291460
  41.2 28.4 %collective-permute-start.13 = (f32[128,8192]{1,0:T(8,128)S(1)}, f32[128,8192]{1,0:T(8,128)S(1)}, u32[]{:S(2)}, u32[]{:S(2)}) collective-permute-start(f32[128,8192]{1,0:T(8,128)S(1)} %copy-done.1), channel_id=1, source_target_pairs={{0,8},{8,0},{1,9},{9,1},{2,10},{10,2},{3,11},{11,3},{4,12},{12,4},... | collective-permute-start | bytes 12582920 | tf_op jit(solution)/shard_map/ppermute | solution.py:382
  41.5 28.1 %collective-permute-start.12 = (f32[128,4096]{1,0:T(8,128)S(1)}, f32[128,4096]{1,0:T(8,128)S(1)}, u32[]{:S(2)}, u32[]{:S(2)}) collective-permute-start(f32[128,4096]{1,0:T(8,128)S(1)} %bitcast.25), channel_id=1, source_target_pairs={{0,8},{8,0},{1,9},{9,1},{2,10},{10,2},{3,11},{11,3},{4,12},{12,4},... | collective-permute-start | bytes 6291464 | tf_op jit(solution)/shard_map/ppermute | solution.py:382
  67.6 2.0 %collective-permute-start.10 = (f32[520,128]{1,0:T(8,128)S(1)}, f32[520,128]{1,0:T(8,128)S(1)}, u32[]{:S(2)}, u32[]{:S(2)}) collective-permute-start(f32[520,128]{1,0:T(8,128)S(1)} %pick_h.1.sent_ref), channel_id=1, source_target_pairs={{0,8},{8,0},{1,9},{9,1},{2,10},{10,2},{3,11},{11,3},{4,12},{12,4},... | collective-permute-start | bytes 798728 | tf_op jit(solution)/shard_map/ppermute | solution.py:379
  67.7 1.9 %collective-permute-start.11 = (f32[512,128]{1,0:T(8,128)S(1)}, f32[512,128]{1,0:T(8,128)S(1)}, u32[]{:S(2)}, u32[]{:S(2)}) collective-permute-start(f32[512,128]{1,0:T(8,128)S(1)} %get-tuple-element.16), channel_id=1, source_target_pairs={{0,8},{8,0},{1,9},{9,1},{2,10},{10,2},{3,11},{11,3},{4,12},{12,4},... | collective-permute-start | bytes 786440 | tf_op jit(solution)/shard_map/ppermute | solution.py:381
where the time goes:
time: 111 us; the launch traced here: 109 us
  blocking collectives  57.6 us (52%)
  Pallas kernels  21.1 us (19%)
  starting transfers between devices  20.5 us (18%)
  waiting for transfers between devices  8.3 us (7%)
    all_to_all x1, blocking collectives, local(): lax.all_to_all(part, ('x', 'y'), split_axis=0, concat_axis=0, tiled=True)  32.5 us
    all_to_all x1, blocking collectives, local(): h = lax.all_to_all(h, 'z', split_axis=0, concat_axis=0, tiled=True)  25.1 us
    ppermute x6, starting transfers between devices, turn(): lax.ppermute(value, axis, [(i, (i + distance) % n) for i in range(n)])  10.1 us
    all_to_all x1, starting transfers between devices, local(): lax.all_to_all(u, 'z', split_axis=0, concat_axis=0, tiled=True)  8.48 us
    pallas_call x1, Pallas kernels, gradients(): pl.pallas_call(functools.partial(gradients_kernel, kcount, scale), in_spe...  6.22 us
    ppermute x6, waiting for transfers between devices, turn(): lax.ppermute(value, axis, [(i, (i + distance) % n) for i in range(n)])  5.41 us
    pallas_call x1, Pallas kernels, back(): pl.pallas_call(functools.partial(back_kernel, kcount, ways), in_specs=[SC...  5.18 us
    pallas_call x1, Pallas kernels, mixed(): pl.pallas_call(mixed_kernel, in_specs=[ANYWHERE, ANYWHERE], out_specs=WHO...  4.82 us
  transfers between devices with their start and end apart: 15, of which 7 were waited for; matrix products, arithmetic and copies ran while one was open for 0% of the time, Pallas kernels for 9%

commit v1 on v0

--- a/solution.py
+++ b/solution.py
@@ -86,7 +86,7 @@
             pltpu.SemaphoreType.DMA((2, pieces)),
             pltpu.SemaphoreType.DMA((pieces,)),
         ],
-        compiler_params=pltpu.CompilerParams(vmem_limit_bytes=16 * MIB),
+        compiler_params=pltpu.CompilerParams(vmem_limit_bytes=20 * MIB),
         name="signal",
     )(tokens, emission, betas)
 
@@ -135,7 +135,7 @@
 
 
 def back_kernel(kcount, ways, place_ref, *refs):
-    slots = len(ways[0])
+    slots = len(ways)
     rights, refs = (refs[:slots], refs[slots : 2 * slots]), refs[2 * slots :]
     signal_ref, u_ref, h_ref, send_ref, g_ref, right_ref, held_ref, sem = refs
     lanes = u_ref.shape[1]
@@ -145,8 +145,7 @@
     for step in range(steps):
         columns = pl.ds(step * share, share)
         waits.append(start(signal_ref.at[:, columns], g_ref.at[:, columns], sem.at[step]))
-    nx, ny = slots, len(ways[1])
-    chips = nx * ny
+    chips = slots * slots
     width = g_ref.shape[1] // kcount
     pieces = width // lanes
     krows = 4 * kcount
@@ -154,11 +153,15 @@
     core = place_ref[2]
     for side in range(2):
         owner = core if side == 0 else 1 - core
-        for a, dx in enumerate(ways[0]):
-            for b, dy in enumerate(ways[1]):
-                x = lax.rem(place_ref[0] + (nx - dx), nx)
-                y = lax.rem(place_ref[1] + (ny - dy), ny)
-                chip = pl.multiple_of((x * ny + y) * rrows, rrows)
+        on_x = owner == 0
+        late = jnp.where(on_x, place_ref[0], place_ref[1])
+        early = jnp.where(on_x, place_ref[1], place_ref[0])
+        for a, da in enumerate(ways):
+            for b, db in enumerate(ways):
+                first = lax.rem(late + (slots - da), slots)
+                second = lax.rem(early + (slots - db), slots)
+                x, y = jnp.where(on_x, first, second), jnp.where(on_x, second, first)
+                chip = pl.multiple_of((x * slots + y) * rrows, rrows)
                 right_ref[owner, pl.ds(chip, rrows), :] = rights[side][a][b * rrows : (b + 1) * rrows, :]
 
     part = 2 * kcount
@@ -217,7 +220,7 @@
             pltpu.VMEM(u.shape, F32),
             pltpu.SemaphoreType.DMA((4,)),
         ],
-        compiler_params=pltpu.CompilerParams(vmem_limit_bytes=16 * MIB),
+        compiler_params=pltpu.CompilerParams(vmem_limit_bytes=20 * MIB),
         name="back",
     )(place, *rights, *others, own, u)
 
@@ -248,7 +251,7 @@
 
 
 def gradients_kernel(kcount, scale, place_ref, h_ref, sent_ref, got_ref, u_ref, uo_ref, *refs):
-    rows_refs, g_refs, (out_ref, rows_ref, g_ref, rows_sem, g_sem) = refs[:2], refs[2:4], refs[4:]
+    rows_refs, g_refs, (out_ref, rows_ref, g_ref, held_ref, rows_sem, g_sem) = refs[:2], refs[2:4], refs[4:]
     blocks, both, width = rows_ref.shape
     lanes = both // 2
     rows_waits, g_waits = [], []
@@ -271,6 +274,8 @@
     last = sent_ref.shape[0] - 8
     weights = [scale / sent_ref[last : last + 1, :], scale / got_ref[last : last + 1, :]]
 
+    side = round(chips**0.5)
+    spots = [jnp.where(core == 0, chip, chip % side * side + chip // side) for chip in range(chips)]
     keep = pl.multiple_of(core * 8, 8)
     for i in range(blocks):
         own = jnp.concatenate([h_ref[z, pl.ds(i * 16 + keep, 8), :] for z in range(zs)], axis=0)
@@ -283,12 +288,11 @@
         for chip in range(chips):
             for piece in range(pieces):
                 first = (i * pieces + piece) * depth
-                out_ref[chip, first : first + depth, :] = grad[
+                out_ref[spots[chip], first : first + depth, :] = grad[
                     chip * depth : (chip + 1) * depth, piece * lanes : (piece + 1) * lanes
                 ]
 
     middle = out_rows // 2
-    flat_ref = out_ref.reshape(chips * out_rows, lanes)
     g_width = g_ref.shape[1] // kcount
     g_pieces = g_width // lanes
     for k in range(kcount):
@@ -311,8 +315,10 @@
         grad = dot3(u, g_ref[:, k * g_width : (k + 1) * g_width], NN)
         for e in range(2):
             for piece in range(g_pieces):
-                place = pl.ds(middle + (k * g_pieces + piece) * 2 + e, chips, stride=out_rows)
-                flat_ref[place, :] = grad[e * chips : (e + 1) * chips, piece * lanes : (piece + 1) * lanes]
+                place = pl.ds((k * g_pieces + piece) * 2 + e, chips, stride=middle)
+                held_ref[place, :] = grad[e * chips : (e + 1) * chips, piece * lanes : (piece + 1) * lanes]
+    for chip in range(chips):
+        out_ref[spots[chip], middle:, :] = held_ref[chip * middle : (chip + 1) * middle, :]
 
 
 def gradients(place, h, sent, got, u, u_other, alphas, g, chips, kcount, blocks, scale):
@@ -328,19 +334,43 @@
         scratch_shapes=[
             pltpu.VMEM((blocks, 2 * rows, states_in // blocks), F32),
             pltpu.VMEM((2 * rows, states), F32),
+            pltpu.VMEM((chips * out_rows // 2, LANES), F32),
             pltpu.SemaphoreType.DMA((2, blocks)),
             pltpu.SemaphoreType.DMA((2, steps)),
         ],
-        compiler_params=pltpu.CompilerParams(vmem_limit_bytes=16 * MIB),
+        compiler_params=pltpu.CompilerParams(vmem_limit_bytes=20 * MIB),
         name="gradients",
     )(place, h, sent, got, u, u_other, *alphas, *g)
 
 
-def turn(value, axis, distance):
+def along(stage, core):
+    return (stage + core) % 2
+
+
+def members(nx, ny, stage):
+    index = lambda x, y, c: (x * ny + y) * 2 + c
+    groups = []
+    for c in range(2):
+        if along(stage, c) == 0:
+            groups += [[index(x, y, c) for x in range(nx)] for y in range(ny)]
+        else:
+            groups += [[index(x, y, c) for y in range(ny)] for x in range(nx)]
+    return groups
+
+
+def turn(value, groups, distance):
     if distance == 0:
         return value
-    n = lax.axis_size(axis)
-    return lax.ppermute(value, axis, [(i, (i + distance) % n) for i in range(n)])
+    pairs = [(line[n], line[(n + distance) % len(line)]) for line in groups for n in range(len(line))]
+    return lax.ppermute(value, ("x", "y", "c"), pairs)
+
+
+def scatter(value, groups):
+    parts = lax.all_to_all(
+        value, ("x", "y", "c"), split_axis=0, concat_axis=0, axis_index_groups=groups, tiled=True
+    )
+    n = len(groups[0])
+    return jnp.sum(parts.reshape(n, value.shape[0] // n, *value.shape[1:]), axis=0)
 
 
 def local(alphas, betas, token_ids, emission, left_blocks, right_blocks):
@@ -361,13 +391,15 @@
 
     right_rows = right_blocks.reshape(kcount, rows_right, pieces, LANES).transpose(0, 2, 1, 3)
     right_rows = right_rows.reshape(kcount * pieces * rows_right, LANES)
-    ways = tuple((0, 1, n - 1) + tuple(range(2, n - 1)) for n in (lax.axis_size("x"), lax.axis_size("y")))
-    right_y = jnp.concatenate([turn(right_rows, "y", d) for d in ways[1]], axis=0)
+    side = lax.axis_size("x")
+    lines = [members(side, side, stage) for stage in range(2)]
+    ways = (0, 1, side - 1) + tuple(range(2, side - 1))
+    right_y = jnp.concatenate([turn(right_rows, lines[1], d) for d in ways], axis=0)
 
     u = mixed(in_hbm(alphas), in_hbm(left_blocks), zs)
     u, right_y = lax.optimization_barrier((u, right_y))
     u = lax.all_to_all(u, "z", split_axis=0, concat_axis=0, tiled=True).reshape(-1, rows)
-    rights = [turn(right_y, "x", d) for d in ways[0]]
+    rights = [turn(right_y, lines[0], d) for d in ways]
     g_own = signal(token_ids, in_hbm(emission), betas)
     rights[1], g_own = lax.optimization_barrier((rights[1], g_own))
     others = [swap(part) for part in rights]
@@ -381,8 +413,7 @@
     u_other = swap(u_sent)
     two_alphas, two_g = (in_hbm(alphas), swap(alphas)), (in_hbm(g_later), swap(g_later))
     part = gradients(place, h, sent, got, u, u_other, two_alphas, two_g, chips, kcount, blocks, scale)
-    parts = lax.all_to_all(part, ("x", "y"), split_axis=0, concat_axis=0, tiled=True)
-    total = jnp.sum(parts, axis=0)
+    total = scatter(scatter(part, lines[0]), lines[1])[0]
     middle = total.shape[0] // 2
     left_grad = total[:middle].reshape(blocks, pieces, -1, LANES).transpose(0, 2, 1, 3).reshape(blocks, -1, width)
     right_grad = total[middle:].reshape(kcount, pieces, rows_right, LANES).transpose(0, 2, 1, 3)

time: 111 us -> 105 us (0.946); the launches traced: 109 us -> 105 us
  blocking collectives: 57.6 us -> 54.2 us
  waiting for transfers between devices: 8.3 us -> 6.97 us
    ppermute x6, waiting for transfers between devices: 5.41 us -> 2.35 us  [turn(): return lax.ppermute(value, ('x', 'y', 'c'), pairs)]
    all_to_all x1 -> x2, blocking collectives: 32.5 us -> 30.6 us  [scatter(): lax.all_to_all(value, ('x', 'y', 'c'), split_axis=0, concat_axis=0, axis_...]
    all_to_all x1, waiting for transfers between devices: 0.16 us -> 1.89 us  [local(): lax.all_to_all(u, 'z', split_axis=0, concat_axis=0, tiled=True)]
    all_to_all x1, blocking collectives: 25.1 us -> 23.6 us  [local(): h = lax.all_to_all(h, 'z', split_axis=0, concat_axis=0, tiled=True)]
  transfers between devices with their start and end apart: 15 -> 15, of which waited for: 7 -> 6; matrix products, arithmetic and copies ran while one was open for 0% -> 0% of each run, Pallas kernels for 9% -> 9%
where the time goes in v1:
time: 105 us
  blocking collectives  54.2 us (52%)
  Pallas kernels  21.4 us (20%)
  starting transfers between devices  20.7 us (20%)
  waiting for transfers between devices  6.97 us (7%)
    all_to_all x2, blocking collectives, scatter(): lax.all_to_all(value, ('x', 'y', 'c'), split_axis=0, concat_axis=0, axis_...  30.6 us
    all_to_all x1, blocking collectives, local(): h = lax.all_to_all(h, 'z', split_axis=0, concat_axis=0, tiled=True)  23.6 us
    ppermute x6, starting transfers between devices, turn(): return lax.ppermute(value, ('x', 'y', 'c'), pairs)  10.1 us
    all_to_all x1, starting transfers between devices, local(): lax.all_to_all(u, 'z', split_axis=0, concat_axis=0, tiled=True)  8.48 us
    pallas_call x1, Pallas kernels, gradients(): pl.pallas_call(functools.partial(gradients_kernel, kcount, scale), in_spe...  6.44 us
    pallas_call x1, Pallas kernels, back(): pl.pallas_call(functools.partial(back_kernel, kcount, ways), in_specs=[SC...  5.26 us
    pallas_call x1, Pallas kernels, mixed(): pl.pallas_call(mixed_kernel, in_specs=[ANYWHERE, ANYWHERE], out_specs=WHO...  4.83 us
    pallas_call x1, Pallas kernels, signal(): pl.pallas_call(signal_kernel, in_specs=[pl.BlockSpec(memory_space=pltpu.V...  4.33 us
  transfers between devices with their start and end apart: 15, of which 6 were waited for; matrix products, arithmetic and copies ran while one was open for 0% of the time, Pallas kernels for 9%

profile of v1, /device:TPU:2, one launch (start us, length us, event | category | flops | bytes accessed | tf_op | source)
XLA Modules:
  0.0 105.1 jit_solution(2625145890741898458)
XLA Ops:
  0.6 3.3 %collective-permute-start.2 = (f32[128,128]{1,0:T(8,128)}, f32[128,128]{1,0:T(8,128)S(1)}, u32[]{:S(2)}, u32[]{:S(2)}) collective-permute-start(f32[128,128]{1,0:T(8,128)} %bitcast.33), channel_id=1, source_target_pairs={{0,32},{16,48},{32,0},{48,16},{64,96},{80,112},{96,64},{112,80},{1... | collective-permute-start | bytes 196616 | tf_op jit(solution)/shard_map/ppermute | solution.py:365
  3.9 1.1 %collective-permute-start.1 = (f32[128,128]{1,0:T(8,128)}, f32[128,128]{1,0:T(8,128)S(1)}, u32[]{:S(2)}, u32[]{:S(2)}) collective-permute-start(f32[128,128]{1,0:T(8,128)} %bitcast.34), channel_id=1, source_target_pairs={{0,48},{16,0},{32,16},{48,32},{64,112},{80,64},{96,80},{112,96},{1... | collective-permute-start | bytes 196616 | tf_op jit(solution)/shard_map/ppermute | solution.py:365
  5.0 1.0 collective-permute-start
  5.9 0.0 copy-start.3
  5.9 0.0 copy-start
  5.9 4.8 %mixed.1 = f32[8,128,128]{2,1,0:T(8,128)} custom-call(f32[128,4096]{1,0:T(8,128)} %bitcast.25, f32[8,128,512]{2,1,0:T(8,128)} %left_hbm.1), custom_call_target="tpu_custom_call" | custom-call | tf_op jit(solution)/shard_map/mixed/pallas_call | solution.py:118
  10.8 0.0 collective-permute-done.2
  10.8 0.0 collective-permute-done.1
  10.8 0.0 collective-permute-done
  10.8 0.0 copy-done.3
  10.9 8.5 %all-to-all-start = ((f32[8,128,128]{2,1,0:T(8,128)}), f32[8,128,128]{2,1,0:T(8,128)S(1)}, u32[]{:S(2)}, u32[]{:S(2)}) async-start(f32[8,128,128]{2,1,0:T(8,128)} %mixed.1), calls=%async_computation | async-start | bytes 1048576 | tf_op jit(solution)/shard_map/all_to_all | solution.py:401
  19.3 1.5 %collective-permute-start.3 = (f32[512,128]{1,0:T(8,128)S(1)}, f32[512,128]{1,0:T(8,128)S(1)}, u32[]{:S(2)}, u32[]{:S(2)}) collective-permute-start(f32[512,128]{1,0:T(8,128)S(1)} %pad_maximum_fusion.refs_0_), channel_id=1, source_target_pairs={{0,64},{64,128},{128,192},{192,0},{16,80},{80,144},{144,208},{208,... | collective-permute-start | bytes 786440 | tf_op jit(solution)/shard_map/ppermute | solution.py:365
  20.8 1.1 %collective-permute-start.5 = (f32[512,128]{1,0:T(8,128)S(1)}, f32[512,128]{1,0:T(8,128)S(1)}, u32[]{:S(2)}, u32[]{:S(2)}) collective-permute-start(f32[512,128]{1,0:T(8,128)S(1)} %pad_maximum_fusion.refs_0_), channel_id=1, source_target_pairs={{0,128},{64,192},{128,0},{192,64},{16,144},{80,208},{144,16},{208,... | collective-permute-start | bytes 786440 | tf_op jit(solution)/shard_map/ppermute | solution.py:365
  21.9 2.2 %collective-permute-start.4 = (f32[512,128]{1,0:T(8,128)S(1)}, f32[512,128]{1,0:T(8,128)S(1)}, u32[]{:S(2)}, u32[]{:S(2)}) collective-permute-start(f32[512,128]{1,0:T(8,128)S(1)} %pad_maximum_fusion.refs_0_), channel_id=1, source_target_pairs={{0,192},{64,0},{128,64},{192,128},{16,208},{80,16},{144,80},{208,1... | collective-permute-start | bytes 786440 | tf_op jit(solution)/shard_map/ppermute | solution.py:365
  24.1 0.0 copy-done
  24.1 4.3 %signal.1.refs_8_.refs_2_ = f32[128,8192]{1,0:T(8,128)} custom-call(s32[2,64]{1,0:T(2,128)S(1)} %copy-done, f32[32,8192]{1,0:T(8,128)} %emission_ref.1, f32[128,8192]{1,0:T(8,128)} %bitcast.29), custom_call_target="tpu_custom_call" | custom-call | tf_op jit(solution)/shard_map/signal/pallas_call | solution.py:78
  28.4 0.1 collective-permute-start.6
  28.5 0.0 collective-permute-done.3.refs_1_
  28.5 0.3 collective-permute-done.5.refs_3_
  28.8 0.2 collective-permute-start.9
  29.0 2.1 %collective-permute-done.4.refs_2_ = f32[512,128]{1,0:T(8,128)S(1)} collective-permute-done((f32[512,128]{1,0:T(8,128)S(1)}, f32[512,128]{1,0:T(8,128)S(1)}, u32[]{:S(2)}, u32[]{:S(2)}) %collective-permute-start.4) | collective-permute-done | bytes 262176 | tf_op jit(solution)/shard_map/ppermute | solution.py:365
  31.1 0.0 collective-permute-start.8
  31.1 0.5 collective-permute-start.7
  31.6 0.1 pad_add_fusion.place_ref
  31.7 0.0 collective-permute-done.6.refs_4_
  31.7 0.0 collective-permute-done.9.refs_7_
  31.7 0.9 collective-permute-done.8.refs_6_
  32.7 0.4 collective-permute-done.7.refs_5_
  33.0 1.9 %all-to-all-done = f32[8,128,128]{2,1,0:T(8,128)S(1)} async-done(((f32[8,128,128]{2,1,0:T(8,128)}), f32[8,128,128]{2,1,0:T(8,128)S(1)}, u32[]{:S(2)}, u32[]{:S(2)}) %all-to-all-start) | async-done | bytes 524320 | tf_op jit(solution)/shard_map/all_to_all | solution.py:401
  34.9 0.0 copy-start.1
  34.9 0.0 copy-start.2
  34.9 5.3 %back.1 = (f32[8,136,128]{2,1,0:T(8,128)S(1)}, f32[512,128]{1,0:T(8,128)S(1)}) custom-call(s32[3]{0:T(128)S(1)} %pad_add_fusion.place_ref, f32[512,128]{1,0:T(8,128)S(1)} %pad_maximum_fusion.refs_0_, f32[512,128]{1,0:T(8,128)S(1)} %collective-permute-done.3.refs_1_, f32[512,128]{1,0:T(8,128)S(1)} %collective-permute-done.4.refs_2_, ...), custom_call_target="tpu_custom_call" | custom-call | tf_op jit(solution)/shard_map/back/pallas_call | solution.py:209
  40.2 0.0 copy-done.1
  40.2 0.3 collective-permute-start.13
  40.5 0.0 copy-done.2
  40.5 0.5 collective-permute-start.12
  41.0 23.6 %all_to_all.20.h_ref = f32[8,136,128]{2,1,0:T(8,128)S(1)} all-to-all(f32[8,136,128]{2,1,0:T(8,128)S(1)} %get-tuple-element.15), channel_id=1, replica_groups=mesh['x'=4,'y'=4,'c'=2,'z'=8] {'z'}, dimensions={0} | all-to-all | bytes 1114112 | tf_op jit(solution)/shard_map/all_to_all | solution.py:409
  64.6 0.6 pick_h.1.sent_ref
  65.2 0.1 collective-permute-start.10
  65.3 0.5 collective-permute-start.11
  65.8 1.4 %collective-permute-done.11.uo_ref = f32[512,128]{1,0:T(8,128)S(1)} collective-permute-done((f32[512,128]{1,0:T(8,128)S(1)}, f32[512,128]{1,0:T(8,128)S(1)}, u32[]{:S(2)}, u32[]{:S(2)}) %collective-permute-start.11) | collective-permute-done | bytes 262176 | tf_op jit(solution)/shard_map/ppermute | solution.py:413
  67.2 0.0 collective-permute-done.12.refs_1_
  67.2 0.0 collective-permute-done.10.got_ref
  67.2 0.0 collective-permute-done.13.refs_3_
  67.2 6.4 %gradients.1 = f32[16,256,128]{2,1,0:T(8,128)S(1)} custom-call(s32[3]{0:T(128)S(1)} %pad_add_fusion.place_ref, f32[8,136,128]{2,1,0:T(8,128)S(1)} %all_to_all.20.h_ref, f32[520,128]{1,0:T(8,128)S(1)} %pick_h.1.sent_ref, f32[520,128]{1,0:T(8,128)S(1)} %collective-permute-done.10.got_ref, f32[1024,128]{1,0:T(8,128)S(1)} %bitcast.24, ...), custom_call_target="tpu_custom_call" | custom-call | tf_op jit(solution)/shard_map/gradients/pallas_call | solution.py:329
  73.6 19.2 %all_to_all.21 = f32[16,256,128]{2,1,0:T(8,128)S(1)} all-to-all(f32[16,256,128]{2,1,0:T(8,128)S(1)} %gradients.1), channel_id=1, replica_groups={{0,64,128,192},{16,80,144,208},{32,96,160,224},{48,112,176,240},{8,24,4..., dimensions={0} | all-to-all | bytes 4194304 | tf_op jit(solution)/shard_map/all_to_all | solution.py:369
  92.8 0.1 reduce_sum.20
  93.0 11.4 %all_to_all.22 = f32[4,256,128]{2,1,0:T(8,128)S(1)} all-to-all(f32[4,256,128]{2,1,0:T(8,128)S(1)} %reduce_sum.20), channel_id=1, replica_groups={{0,16,32,48},{64,80,96,112},{128,144,160,176},{192,208,224,240},{8,72,1..., dimensions={0} | all-to-all | bytes 1048576 | tf_op jit(solution)/shard_map/all_to_all | solution.py:369
  104.4 0.7 fusion
  (2 shorter events, 0.0 us)
Async XLA Ops:
  0.6 10.2 %collective-permute-start.2 = (f32[128,128]{1,0:T(8,128)}, f32[128,128]{1,0:T(8,128)S(1)}, u32[]{:S(2)}, u32[]{:S(2)}) collective-permute-start(f32[128,128]{1,0:T(8,128)} %bitcast.33), channel_id=1, source_target_pairs={{0,32},{16,48},{32,0},{48,16},{64,96},{80,112},{96,64},{112,80},{1... | collective-permute-start | bytes 196616 | tf_op jit(solution)/shard_map/ppermute | solution.py:365
  3.9 6.9 %collective-permute-start.1 = (f32[128,128]{1,0:T(8,128)}, f32[128,128]{1,0:T(8,128)S(1)}, u32[]{:S(2)}, u32[]{:S(2)}) collective-permute-start(f32[128,128]{1,0:T(8,128)} %bitcast.34), channel_id=1, source_target_pairs={{0,48},{16,0},{32,16},{48,32},{64,112},{80,64},{96,80},{112,96},{1... | collective-permute-start | bytes 196616 | tf_op jit(solution)/shard_map/ppermute | solution.py:365
  5.0 5.8 %collective-permute-start = (f32[128,128]{1,0:T(8,128)}, f32[128,128]{1,0:T(8,128)S(1)}, u32[]{:S(2)}, u32[]{:S(2)}) collective-permute-start(f32[128,128]{1,0:T(8,128)} %bitcast.35), channel_id=1, source_target_pairs={{0,16},{16,32},{32,48},{48,0},{64,80},{80,96},{96,112},{112,64},{1... | collective-permute-start | bytes 196616 | tf_op jit(solution)/shard_map/ppermute | solution.py:365
  5.9 4.9 %copy-start.3 = (f32[16,2,512]{2,1,0:T(2,128)S(1)}, f32[16,2,512]{2,1,0:T(2,128)}, u32[]{:S(2)}) copy-start(f32[16,2,512]{2,1,0:T(2,128)} %param.11) | copy-start | bytes 196612
  5.9 18.1 %copy-start = (s32[2,64]{1,0:T(2,128)S(1)}, s32[2,64]{1,0:T(2,128)}, u32[]{:S(2)}) copy-start(s32[2,64]{1,0:T(2,128)} %tok_ref.1) | copy-start | bytes 1540
  10.9 24.1 %all-to-all-start = ((f32[8,128,128]{2,1,0:T(8,128)}), f32[8,128,128]{2,1,0:T(8,128)S(1)}, u32[]{:S(2)}, u32[]{:S(2)}) async-start(f32[8,128,128]{2,1,0:T(8,128)} %mixed.1), calls=%async_computation | async-start | bytes 1048576 | tf_op jit(solution)/shard_map/all_to_all | solution.py:401
  19.3 9.2 %collective-permute-start.3 = (f32[512,128]{1,0:T(8,128)S(1)}, f32[512,128]{1,0:T(8,128)S(1)}, u32[]{:S(2)}, u32[]{:S(2)}) collective-permute-start(f32[512,128]{1,0:T(8,128)S(1)} %pad_maximum_fusion.refs_0_), channel_id=1, source_target_pairs={{0,64},{64,128},{128,192},{192,0},{16,80},{80,144},{144,208},{208,... | collective-permute-start | bytes 786440 | tf_op jit(solution)/shard_map/ppermute | solution.py:365
  20.8 8.0 %collective-permute-start.5 = (f32[512,128]{1,0:T(8,128)S(1)}, f32[512,128]{1,0:T(8,128)S(1)}, u32[]{:S(2)}, u32[]{:S(2)}) collective-permute-start(f32[512,128]{1,0:T(8,128)S(1)} %pad_maximum_fusion.refs_0_), channel_id=1, source_target_pairs={{0,128},{64,192},{128,0},{192,64},{16,144},{80,208},{144,16},{208,... | collective-permute-start | bytes 786440 | tf_op jit(solution)/shard_map/ppermute | solution.py:365
  21.9 9.2 %collective-permute-start.4 = (f32[512,128]{1,0:T(8,128)S(1)}, f32[512,128]{1,0:T(8,128)S(1)}, u32[]{:S(2)}, u32[]{:S(2)}) collective-permute-start(f32[512,128]{1,0:T(8,128)S(1)} %pad_maximum_fusion.refs_0_), channel_id=1, source_target_pairs={{0,192},{64,0},{128,64},{192,128},{16,208},{80,16},{144,80},{208,1... | collective-permute-start | bytes 786440 | tf_op jit(solution)/shard_map/ppermute | solution.py:365
  28.4 3.3 %collective-permute-start.6 = (f32[512,128]{1,0:T(8,128)S(1)}, f32[512,128]{1,0:T(8,128)S(1)}, u32[]{:S(2)}, u32[]{:S(2)}) collective-permute-start(f32[512,128]{1,0:T(8,128)S(1)} %pad_maximum_fusion.refs_0_), channel_id=1, source_target_pairs={{0,8},{8,0},{1,9},{9,1},{2,10},{10,2},{3,11},{11,3},{4,12},{12,4},... | collective-permute-start | bytes 786440 | tf_op jit(solution)/shard_map/ppermute | solution.py:405
  28.8 2.9 %collective-permute-start.9 = (f32[512,128]{1,0:T(8,128)S(1)}, f32[512,128]{1,0:T(8,128)S(1)}, u32[]{:S(2)}, u32[]{:S(2)}) collective-permute-start(f32[512,128]{1,0:T(8,128)S(1)} %collective-permute-done.5.refs_3_), channel_id=1, source_target_pairs={{0,8},{8,0},{1,9},{9,1},{2,10},{10,2},{3,11},{11,3},{4,12},{12,4},... | collective-permute-start | bytes 786440 | tf_op jit(solution)/shard_map/ppermute | solution.py:405
  31.1 1.5 %collective-permute-start.8 = (f32[512,128]{1,0:T(8,128)S(1)}, f32[512,128]{1,0:T(8,128)S(1)}, u32[]{:S(2)}, u32[]{:S(2)}) collective-permute-start(f32[512,128]{1,0:T(8,128)S(1)} %collective-permute-done.4.refs_2_), channel_id=1, source_target_pairs={{0,8},{8,0},{1,9},{9,1},{2,10},{10,2},{3,11},{11,3},{4,12},{12,4},... | collective-permute-start | bytes 786440 | tf_op jit(solution)/shard_map/ppermute | solution.py:405
  31.1 1.9 %collective-permute-start.7 = (f32[512,128]{1,0:T(8,128)S(1)}, f32[512,128]{1,0:T(8,128)S(1)}, u32[]{:S(2)}, u32[]{:S(2)}) collective-permute-start(f32[512,128]{1,0:T(8,128)S(1)} %collective-permute-done.3.refs_1_), channel_id=1, source_target_pairs={{0,8},{8,0},{1,9},{9,1},{2,10},{10,2},{3,11},{11,3},{4,12},{12,4},... | collective-permute-start | bytes 786440 | tf_op jit(solution)/shard_map/ppermute | solution.py:405
  34.9 5.3 %copy-start.1 = (f32[128,8192]{1,0:T(8,128)S(1)}, f32[128,8192]{1,0:T(8,128)}, u32[]{:S(2)}) copy-start(f32[128,8192]{1,0:T(8,128)} %signal.1.refs_8_.refs_2_) | copy-start | bytes 12582916
  34.9 5.6 %copy-start.2 = (f32[2,64,4096]{2,1,0:T(8,128)S(1)}, f32[2,64,4096]{2,1,0:T(8,128)}, u32[]{:S(2)}) copy-start(f32[2,64,4096]{2,1,0:T(8,128)} %param.6) | copy-start | bytes 6291460
  40.2 27.0 %collective-permute-start.13 = (f32[128,8192]{1,0:T(8,128)S(1)}, f32[128,8192]{1,0:T(8,128)S(1)}, u32[]{:S(2)}, u32[]{:S(2)}) collective-permute-start(f32[128,8192]{1,0:T(8,128)S(1)} %copy-done.1), channel_id=1, source_target_pairs={{0,8},{8,0},{1,9},{9,1},{2,10},{10,2},{3,11},{11,3},{4,12},{12,4},... | collective-permute-start | bytes 12582920 | tf_op jit(solution)/shard_map/ppermute | solution.py:414
  40.5 26.7 %collective-permute-start.12 = (f32[128,4096]{1,0:T(8,128)S(1)}, f32[128,4096]{1,0:T(8,128)S(1)}, u32[]{:S(2)}, u32[]{:S(2)}) collective-permute-start(f32[128,4096]{1,0:T(8,128)S(1)} %bitcast.27), channel_id=1, source_target_pairs={{0,8},{8,0},{1,9},{9,1},{2,10},{10,2},{3,11},{11,3},{4,12},{12,4},... | collective-permute-start | bytes 6291464 | tf_op jit(solution)/shard_map/ppermute | solution.py:414
  65.2 2.0 %collective-permute-start.10 = (f32[520,128]{1,0:T(8,128)S(1)}, f32[520,128]{1,0:T(8,128)S(1)}, u32[]{:S(2)}, u32[]{:S(2)}) collective-permute-start(f32[520,128]{1,0:T(8,128)S(1)} %pick_h.1.sent_ref), channel_id=1, source_target_pairs={{0,8},{8,0},{1,9},{9,1},{2,10},{10,2},{3,11},{11,3},{4,12},{12,4},... | collective-permute-start | bytes 798728 | tf_op jit(solution)/shard_map/ppermute | solution.py:411
  65.3 1.9 %collective-permute-start.11 = (f32[512,128]{1,0:T(8,128)S(1)}, f32[512,128]{1,0:T(8,128)S(1)}, u32[]{:S(2)}, u32[]{:S(2)}) collective-permute-start(f32[512,128]{1,0:T(8,128)S(1)} %get-tuple-element.16), channel_id=1, source_target_pairs={{0,8},{8,0},{1,9},{9,1},{2,10},{10,2},{3,11},{11,3},{4,12},{12,4},... | collective-permute-start | bytes 786440 | tf_op jit(solution)/shard_map/ppermute | solution.py:413

commit v2 on v1

--- a/solution.py
+++ b/solution.py
@@ -39,7 +39,7 @@
     return both[:rows] + (part(ah, bl) + both[rows:])
 
 
-def signal_kernel(tok_ref, emission_ref, betas_ref, g_ref, table_ref, held_ref, in_sem, out_sem):
+def signal_kernel(tok_ref, emission_ref, betas_ref, g_ref, held_ref, table_ref, in_sem, out_sem):
     uniq, states = emission_ref.shape
     rows = betas_ref.shape[0]
     pieces = out_sem.shape[0]
@@ -78,11 +78,10 @@
     return pl.pallas_call(
         signal_kernel,
         in_specs=[pl.BlockSpec(memory_space=pltpu.VMEM), ANYWHERE, ANYWHERE],
-        out_specs=ANYWHERE,
-        out_shape=pltpu.HBM(betas.shape, F32),
+        out_specs=(ANYWHERE, WHOLE),
+        out_shape=(pltpu.HBM(betas.shape, F32), jax.ShapeDtypeStruct(betas.shape, F32)),
         scratch_shapes=[
             pltpu.VMEM(emission.shape, F32),
-            pltpu.VMEM(betas.shape, F32),
             pltpu.SemaphoreType.DMA((2, pieces)),
             pltpu.SemaphoreType.DMA((pieces,)),
         ],
@@ -137,14 +136,8 @@
 def back_kernel(kcount, ways, place_ref, *refs):
     slots = len(ways)
     rights, refs = (refs[:slots], refs[slots : 2 * slots]), refs[2 * slots :]
-    signal_ref, u_ref, h_ref, send_ref, g_ref, right_ref, held_ref, sem = refs
+    g_ref, u_ref, h_ref, send_ref, right_ref, held_ref = refs
     lanes = u_ref.shape[1]
-    steps = sem.shape[0]
-    share = g_ref.shape[1] // steps
-    waits = []
-    for step in range(steps):
-        columns = pl.ds(step * share, share)
-        waits.append(start(signal_ref.at[:, columns], g_ref.at[:, columns], sem.at[step]))
     chips = slots * slots
     width = g_ref.shape[1] // kcount
     pieces = width // lanes
@@ -171,8 +164,6 @@
 
     total = jnp.zeros((8, lanes), F32)
     for k in range(kcount):
-        if k * steps % kcount == 0:
-            waits[k * steps // kcount].wait()
         r = jnp.concatenate(
             [
                 jnp.concatenate(
@@ -203,54 +194,27 @@
 
 
 def back(place, ways, rights, others, own, u, zs, kcount):
-    rows, states = own.shape
+    rows = own.shape[0]
     body = u.shape[0] // zs
     right = (2, rights[0].shape[0] * len(rights), rights[0].shape[1])
     return pl.pallas_call(
         functools.partial(back_kernel, kcount, ways),
-        in_specs=[SCALARS, *[WHOLE for _ in (*rights, *others)], ANYWHERE, WHOLE],
+        in_specs=[SCALARS, *[WHOLE for _ in (*rights, *others)], WHOLE, WHOLE],
         out_specs=(WHOLE, WHOLE),
         out_shape=(
             jax.ShapeDtypeStruct((zs, body + 8, rows), F32),
             jax.ShapeDtypeStruct((u.shape[0] // 2, rows), F32),
         ),
         scratch_shapes=[
-            pltpu.VMEM((rows, states), F32),
             pltpu.VMEM(right, F32),
             pltpu.VMEM(u.shape, F32),
-            pltpu.SemaphoreType.DMA((4,)),
         ],
         compiler_params=pltpu.CompilerParams(vmem_limit_bytes=20 * MIB),
         name="back",
     )(place, *rights, *others, own, u)
 
 
-def pick_h_kernel(place_ref, h_ref, send_ref):
-    zs, height, _ = h_ref.shape
-    first = pl.multiple_of((1 - place_ref[2]) * 8, 8)
-    total = h_ref[0, height - 8 : height, :]
-    for z in range(1, zs):
-        total = total + h_ref[z, height - 8 : height, :]
-    bands = (height - 8) // 16
-    for z in range(zs):
-        for band in range(bands):
-            send_ref[(z * bands + band) * 8 : (z * bands + band + 1) * 8, :] = h_ref[z, pl.ds(band * 16 + first, 8), :]
-    send_ref[zs * bands * 8 :, :] = total
-
-
-def pick_h(place, h):
-    zs, height, lanes = h.shape
-    return pl.pallas_call(
-        pick_h_kernel,
-        in_specs=[SCALARS, WHOLE],
-        out_specs=WHOLE,
-        out_shape=jax.ShapeDtypeStruct((zs * (height - 8) // 2 + 8, lanes), F32),
-        compiler_params=pltpu.CompilerParams(vmem_limit_bytes=4 * MIB),
-        name="pick_h",
-    )(place, h)
-
-
-def gradients_kernel(kcount, scale, place_ref, h_ref, sent_ref, got_ref, u_ref, uo_ref, *refs):
+def gradients_kernel(kcount, scale, place_ref, h_ref, ho_ref, u_ref, uo_ref, *refs):
     rows_refs, g_refs, (out_ref, rows_ref, g_ref, held_ref, rows_sem, g_sem) = refs[:2], refs[2:4], refs[4:]
     blocks, both, width = rows_ref.shape
     lanes = both // 2
@@ -271,15 +235,17 @@
     chips, out_rows, _ = out_ref.shape
     pieces = width // lanes
     zs = h_ref.shape[0]
-    last = sent_ref.shape[0] - 8
-    weights = [scale / sent_ref[last : last + 1, :], scale / got_ref[last : last + 1, :]]
+    weights = []
+    for ref in (h_ref, ho_ref):
+        last = ref.shape[1] - 8
+        weights.append(scale / sum(ref[z, last : last + 1, :] for z in range(zs)))
 
     side = round(chips**0.5)
     spots = [jnp.where(core == 0, chip, chip % side * side + chip // side) for chip in range(chips)]
     keep = pl.multiple_of(core * 8, 8)
     for i in range(blocks):
         own = jnp.concatenate([h_ref[z, pl.ds(i * 16 + keep, 8), :] for z in range(zs)], axis=0)
-        other = jnp.concatenate([got_ref[(z * blocks + i) * 8 : (z * blocks + i + 1) * 8, :] for z in range(zs)], axis=0)
+        other = jnp.concatenate([ho_ref[z, pl.ds(i * 16 + keep, 8), :] for z in range(zs)], axis=0)
         h = jnp.concatenate([own * weights[0], other * weights[1]], axis=1)
         for copy in rows_waits[i]:
             copy.wait()
@@ -321,14 +287,14 @@
         out_ref[spots[chip], middle:, :] = held_ref[chip * middle : (chip + 1) * middle, :]
 
 
-def gradients(place, h, sent, got, u, u_other, alphas, g, chips, kcount, blocks, scale):
+def gradients(place, h, h_other, u, u_other, alphas, g, chips, kcount, blocks, scale):
     rows, states_in = alphas[0].shape
     states = g[0].shape[1]
     out_rows = (blocks // 2 * (states_in // blocks) * kcount * h.shape[0] + 2 * states * chips) // LANES // chips
     steps = 4
     return pl.pallas_call(
         functools.partial(gradients_kernel, kcount, scale),
-        in_specs=[SCALARS] + [WHOLE] * 5 + [ANYWHERE] * 4,
+        in_specs=[SCALARS] + [WHOLE] * 4 + [ANYWHERE] * 4,
         out_specs=WHOLE,
         out_shape=jax.ShapeDtypeStruct((chips, out_rows, LANES), F32),
         scratch_shapes=[
@@ -340,7 +306,7 @@
         ],
         compiler_params=pltpu.CompilerParams(vmem_limit_bytes=20 * MIB),
         name="gradients",
-    )(place, h, sent, got, u, u_other, *alphas, *g)
+    )(place, h, h_other, u, u_other, *alphas, *g)
 
 
 def along(stage, core):
@@ -400,19 +366,17 @@
     u, right_y = lax.optimization_barrier((u, right_y))
     u = lax.all_to_all(u, "z", split_axis=0, concat_axis=0, tiled=True).reshape(-1, rows)
     rights = [turn(right_y, lines[0], d) for d in ways]
-    g_own = signal(token_ids, in_hbm(emission), betas)
+    g_own, g_near = signal(token_ids, in_hbm(emission), betas)
     rights[1], g_own = lax.optimization_barrier((rights[1], g_own))
     others = [swap(part) for part in rights]
 
-    h, u_sent = back(place, ways, rights, others, in_hbm(g_own), u, zs, kcount)
-    h, g_later = lax.optimization_barrier((h, g_own))
+    h, u_sent = back(place, ways, rights, others, g_near, u, zs, kcount)
+    h, g_later = lax.optimization_barrier((h, g_near))
     h = lax.all_to_all(h, "z", split_axis=0, concat_axis=0, tiled=True)
-    sent = pick_h(place, h)
-    got = swap(sent)
-
-    u_other = swap(u_sent)
-    two_alphas, two_g = (in_hbm(alphas), swap(alphas)), (in_hbm(g_later), swap(g_later))
-    part = gradients(place, h, sent, got, u, u_other, two_alphas, two_g, chips, kcount, blocks, scale)
+    h_other, u_other = swap(h), swap(u_sent)
+
+    two_alphas, two_g = (in_hbm(alphas), swap(alphas)), (in_hbm(g_own), swap(g_later))
+    part = gradients(place, h, h_other, u, u_other, two_alphas, two_g, chips, kcount, blocks, scale)
     total = scatter(scatter(part, lines[0]), lines[1])[0]
     middle = total.shape[0] // 2
     left_grad = total[:middle].reshape(blocks, pieces, -1, LANES).transpose(0, 2, 1, 3).reshape(blocks, -1, width)

time: 105 us -> 104 us (level)
  local copies, waits for them, and re-layouts: 0.67 us -> 4.84 us
  Pallas kernels: 21.4 us -> 18.8 us
  blocking collectives: 54.2 us -> 53 us
    unnamed x8 -> x10, local copies, waits for them, and re-layouts: 0.01 us -> 4.18 us
    ppermute x6, waiting for transfers between devices: 2.35 us -> 0.22 us  [turn(): return lax.ppermute(value, ('x', 'y', 'c'), pairs)]
    pallas_call x1, Pallas kernels: 5.26 us -> 3.26 us  [back(): pl.pallas_call(functools.partial(back_kernel, kcount, ways), in_specs=[SC...]
  transfers between devices with their start and end apart: 15 -> 15, of which waited for: 6 -> 7; matrix products, arithmetic and copies ran while one was open for 0% -> 0% of each run, Pallas kernels for 9% -> 9%
where the time goes in v2:
time: 104 us
  blocking collectives  53 us (51%)
  starting transfers between devices  20 us (19%)
  Pallas kernels  18.8 us (18%)
  waiting for transfers between devices  6.03 us (6%)
  local copies, waits for them, and re-layouts  4.84 us (5%)
    all_to_all x2, blocking collectives, scatter(): lax.all_to_all(value, ('x', 'y', 'c'), split_axis=0, concat_axis=0, axis_...  29.9 us
    all_to_all x1, blocking collectives, local(): h = lax.all_to_all(h, 'z', split_axis=0, concat_axis=0, tiled=True)  23.1 us
    ppermute x6, starting transfers between devices, turn(): return lax.ppermute(value, ('x', 'y', 'c'), pairs)  9.45 us
    all_to_all x1, starting transfers between devices, local(): lax.all_to_all(u, 'z', split_axis=0, concat_axis=0, tiled=True)  8.48 us
    pallas_call x1, Pallas kernels, gradients(): pl.pallas_call(functools.partial(gradients_kernel, kcount, scale), in_spe...  6.3 us
    pallas_call x1, Pallas kernels, mixed(): pl.pallas_call(mixed_kernel, in_specs=[ANYWHERE, ANYWHERE], out_specs=WHO...  4.87 us
    pallas_call x1, Pallas kernels, signal(): pl.pallas_call(signal_kernel, in_specs=[pl.BlockSpec(memory_space=pltpu.V...  4.34 us
    unnamed x10, local copies, waits for them, and re-layouts  4.18 us
  transfers between devices with their start and end apart: 15, of which 7 were waited for; matrix products, arithmetic and copies ran while one was open for 0% of the time, Pallas kernels for 9%

profile of v2, /device:TPU:2, one launch (start us, length us, event | category | flops | bytes accessed | tf_op | source)
XLA Modules:
  0.0 103.7 jit_solution(12923483723567856715)
XLA Ops:
  0.6 1.7 %collective-permute-start = (f32[128,128]{1,0:T(8,128)}, f32[128,128]{1,0:T(8,128)S(1)}, u32[]{:S(2)}, u32[]{:S(2)}) collective-permute-start(f32[128,128]{1,0:T(8,128)} %bitcast.33), channel_id=1, source_target_pairs={{0,16},{16,32},{32,48},{48,0},{64,80},{80,96},{96,112},{112,64},{1... | collective-permute-start | bytes 196616 | tf_op jit(solution)/shard_map/ppermute | solution.py:331
  2.3 1.7 %collective-permute-start.1 = (f32[128,128]{1,0:T(8,128)}, f32[128,128]{1,0:T(8,128)S(1)}, u32[]{:S(2)}, u32[]{:S(2)}) collective-permute-start(f32[128,128]{1,0:T(8,128)} %bitcast.34), channel_id=1, source_target_pairs={{0,48},{16,0},{32,16},{48,32},{64,112},{80,64},{96,80},{112,96},{1... | collective-permute-start | bytes 196616 | tf_op jit(solution)/shard_map/ppermute | solution.py:331
  3.9 2.0 %collective-permute-start.2 = (f32[128,128]{1,0:T(8,128)}, f32[128,128]{1,0:T(8,128)S(1)}, u32[]{:S(2)}, u32[]{:S(2)}) collective-permute-start(f32[128,128]{1,0:T(8,128)} %bitcast.35), channel_id=1, source_target_pairs={{0,32},{16,48},{32,0},{48,16},{64,96},{80,112},{96,64},{112,80},{1... | collective-permute-start | bytes 196616 | tf_op jit(solution)/shard_map/ppermute | solution.py:331
  5.9 0.0 copy-start.4
  5.9 0.0 copy-start.2
  5.9 4.9 %mixed.1 = f32[8,128,128]{2,1,0:T(8,128)} custom-call(f32[128,4096]{1,0:T(8,128)} %bitcast.25, f32[8,128,512]{2,1,0:T(8,128)} %left_hbm.1), custom_call_target="tpu_custom_call" | custom-call | tf_op jit(solution)/shard_map/mixed/pallas_call | solution.py:117
  10.8 0.0 collective-permute-done
  10.8 0.0 collective-permute-done.1
  10.8 0.0 collective-permute-done.2
  10.8 0.0 copy-done.4
  10.9 8.5 %all-to-all-start = ((f32[8,128,128]{2,1,0:T(8,128)}), f32[8,128,128]{2,1,0:T(8,128)S(1)}, u32[]{:S(2)}, u32[]{:S(2)}) async-start(f32[8,128,128]{2,1,0:T(8,128)} %mixed.1), calls=%async_computation | async-start | bytes 1048576 | tf_op jit(solution)/shard_map/all_to_all | solution.py:367
  19.4 1.5 %collective-permute-start.3 = (f32[512,128]{1,0:T(8,128)S(1)}, f32[512,128]{1,0:T(8,128)S(1)}, u32[]{:S(2)}, u32[]{:S(2)}) collective-permute-start(f32[512,128]{1,0:T(8,128)S(1)} %pad_maximum_fusion.refs_0_), channel_id=1, source_target_pairs={{0,64},{64,128},{128,192},{192,0},{16,80},{80,144},{144,208},{208,... | collective-permute-start | bytes 786440 | tf_op jit(solution)/shard_map/ppermute | solution.py:331
  20.8 0.5 collective-permute-start.4
  21.4 2.1 %collective-permute-start.5 = (f32[512,128]{1,0:T(8,128)S(1)}, f32[512,128]{1,0:T(8,128)S(1)}, u32[]{:S(2)}, u32[]{:S(2)}) collective-permute-start(f32[512,128]{1,0:T(8,128)S(1)} %pad_maximum_fusion.refs_0_), channel_id=1, source_target_pairs={{0,128},{64,192},{128,0},{192,64},{16,144},{80,208},{144,16},{208,... | collective-permute-start | bytes 786440 | tf_op jit(solution)/shard_map/ppermute | solution.py:331
  23.5 0.0 copy-done.2
  23.5 4.3 %signal.1 = (f32[128,8192]{1,0:T(8,128)}, f32[128,8192]{1,0:T(8,128)S(1)}) custom-call(s32[2,64]{1,0:T(2,128)S(1)} %copy-done.2, f32[32,8192]{1,0:T(8,128)} %emission_ref.1, f32[128,8192]{1,0:T(8,128)} %bitcast.29), custom_call_target="tpu_custom_call" | custom-call | tf_op jit(solution)/shard_map/signal/pallas_call | solution.py:78
  27.9 0.0 copy-start
  27.9 2.0 %copy-done = f32[128,8192]{1,0:T(8,128)} copy-done((f32[128,8192]{1,0:T(8,128)}, f32[128,8192]{1,0:T(8,128)S(1)}, u32[]{:S(2)}) %copy-start) | copy-done | bytes 4194328
  29.9 0.0 collective-permute-start.6
  29.9 0.0 collective-permute-done.3.refs_1_
  29.9 0.5 collective-permute-start.7
  30.4 0.0 collective-permute-done.4.refs_2_
  30.4 0.1 collective-permute-start.8
  30.5 0.2 collective-permute-done.5.refs_3_
  30.7 0.2 collective-permute-start.9
  30.9 0.1 pad_add_fusion.place_ref
  31.0 0.4 collective-permute-done.6.refs_4_
  31.4 0.4 collective-permute-done.7.refs_5_
  31.8 0.4 collective-permute-done.8.refs_6_
  32.1 0.4 collective-permute-done.9.refs_7_
  32.5 2.4 %all-to-all-done = f32[8,128,128]{2,1,0:T(8,128)S(1)} async-done(((f32[8,128,128]{2,1,0:T(8,128)}), f32[8,128,128]{2,1,0:T(8,128)S(1)}, u32[]{:S(2)}, u32[]{:S(2)}) %all-to-all-start) | async-done | bytes 524320 | tf_op jit(solution)/shard_map/all_to_all | solution.py:367
  34.9 0.0 copy-start.1
  34.9 2.2 %copy-done.1 = f32[128,8192]{1,0:T(8,128)S(1)} copy-done((f32[128,8192]{1,0:T(8,128)S(1)}, f32[128,8192]{1,0:T(8,128)}, u32[]{:S(2)}) %copy-start.1) | copy-done | bytes 4194328
  37.1 0.0 copy-start.3
  37.1 3.3 %back.1 = (f32[8,136,128]{2,1,0:T(8,128)S(1)}, f32[512,128]{1,0:T(8,128)S(1)}) custom-call(s32[3]{0:T(128)S(1)} %pad_add_fusion.place_ref, f32[512,128]{1,0:T(8,128)S(1)} %pad_maximum_fusion.refs_0_, f32[512,128]{1,0:T(8,128)S(1)} %collective-permute-done.3.refs_1_, f32[512,128]{1,0:T(8,128)S(1)} %collective-permute-done.4.refs_2_, ...), custom_call_target="tpu_custom_call" | custom-call | tf_op jit(solution)/shard_map/back/pallas_call | solution.py:200
  40.4 0.3 collective-permute-start.13
  40.7 0.0 copy-done.3
  40.7 0.5 collective-permute-start.12
  41.2 23.1 %all_to_all.20.h_ref = f32[8,136,128]{2,1,0:T(8,128)S(1)} all-to-all(f32[8,136,128]{2,1,0:T(8,128)S(1)} %get-tuple-element.18), channel_id=1, replica_groups=mesh['x'=4,'y'=4,'c'=2,'z'=8] {'z'}, dimensions={0} | all-to-all | bytes 1114112 | tf_op jit(solution)/shard_map/all_to_all | solution.py:375
  64.2 0.0 collective-permute-start.10
  64.3 0.5 collective-permute-start.11
  64.8 1.8 %collective-permute-done.11.uo_ref = f32[512,128]{1,0:T(8,128)S(1)} collective-permute-done((f32[512,128]{1,0:T(8,128)S(1)}, f32[512,128]{1,0:T(8,128)S(1)}, u32[]{:S(2)}, u32[]{:S(2)}) %collective-permute-start.11) | collective-permute-done | bytes 262176 | tf_op jit(solution)/shard_map/ppermute | solution.py:376
  66.6 0.0 collective-permute-done.12.refs_1_
  66.6 0.0 collective-permute-done.10.ho_ref
  66.6 0.0 collective-permute-done.13.refs_3_
  66.6 6.3 %gradients.1 = f32[16,256,128]{2,1,0:T(8,128)S(1)} custom-call(s32[3]{0:T(128)S(1)} %pad_add_fusion.place_ref, f32[8,136,128]{2,1,0:T(8,128)S(1)} %all_to_all.20.h_ref, f32[8,136,128]{2,1,0:T(8,128)S(1)} %collective-permute-done.10.ho_ref, f32[1024,128]{1,0:T(8,128)S(1)} %bitcast.24, f32[512,128]{1,0:T(8,128)S(1)} %collective-permute-done.11.uo_ref, ...), custom_call_target="tpu_custom_call" | custom-call | tf_op jit(solution)/shard_map/gradients/pallas_call | solution.py:295
  72.9 19.2 %all_to_all.21 = f32[16,256,128]{2,1,0:T(8,128)S(1)} all-to-all(f32[16,256,128]{2,1,0:T(8,128)S(1)} %gradients.1), channel_id=1, replica_groups={{0,64,128,192},{16,80,144,208},{32,96,160,224},{48,112,176,240},{8,24,4..., dimensions={0} | all-to-all | bytes 4194304 | tf_op jit(solution)/shard_map/all_to_all | solution.py:335
  92.2 0.1 reduce_sum.20
  92.3 10.7 %all_to_all.22 = f32[4,256,128]{2,1,0:T(8,128)S(1)} all-to-all(f32[4,256,128]{2,1,0:T(8,128)S(1)} %reduce_sum.20), channel_id=1, replica_groups={{0,16,32,48},{64,80,96,112},{128,144,160,176},{192,208,224,240},{8,72,1..., dimensions={0} | all-to-all | bytes 1048576 | tf_op jit(solution)/shard_map/all_to_all | solution.py:335
  103.0 0.7 fusion
  (2 shorter events, 0.0 us)
Async XLA Ops:
  0.6 10.2 %collective-permute-start = (f32[128,128]{1,0:T(8,128)}, f32[128,128]{1,0:T(8,128)S(1)}, u32[]{:S(2)}, u32[]{:S(2)}) collective-permute-start(f32[128,128]{1,0:T(8,128)} %bitcast.33), channel_id=1, source_target_pairs={{0,16},{16,32},{32,48},{48,0},{64,80},{80,96},{96,112},{112,64},{1... | collective-permute-start | bytes 196616 | tf_op jit(solution)/shard_map/ppermute | solution.py:331
  2.3 8.5 %collective-permute-start.1 = (f32[128,128]{1,0:T(8,128)}, f32[128,128]{1,0:T(8,128)S(1)}, u32[]{:S(2)}, u32[]{:S(2)}) collective-permute-start(f32[128,128]{1,0:T(8,128)} %bitcast.34), channel_id=1, source_target_pairs={{0,48},{16,0},{32,16},{48,32},{64,112},{80,64},{96,80},{112,96},{1... | collective-permute-start | bytes 196616 | tf_op jit(solution)/shard_map/ppermute | solution.py:331
  3.9 6.9 %collective-permute-start.2 = (f32[128,128]{1,0:T(8,128)}, f32[128,128]{1,0:T(8,128)S(1)}, u32[]{:S(2)}, u32[]{:S(2)}) collective-permute-start(f32[128,128]{1,0:T(8,128)} %bitcast.35), channel_id=1, source_target_pairs={{0,32},{16,48},{32,0},{48,16},{64,96},{80,112},{96,64},{112,80},{1... | collective-permute-start | bytes 196616 | tf_op jit(solution)/shard_map/ppermute | solution.py:331
  5.9 4.9 %copy-start.4 = (f32[16,2,512]{2,1,0:T(2,128)S(1)}, f32[16,2,512]{2,1,0:T(2,128)}, u32[]{:S(2)}) copy-start(f32[16,2,512]{2,1,0:T(2,128)} %param.11) | copy-start | bytes 196612
  5.9 17.6 %copy-start.2 = (s32[2,64]{1,0:T(2,128)S(1)}, s32[2,64]{1,0:T(2,128)}, u32[]{:S(2)}) copy-start(s32[2,64]{1,0:T(2,128)} %tok_ref.1) | copy-start | bytes 1540
  10.9 24.1 %all-to-all-start = ((f32[8,128,128]{2,1,0:T(8,128)}), f32[8,128,128]{2,1,0:T(8,128)S(1)}, u32[]{:S(2)}, u32[]{:S(2)}) async-start(f32[8,128,128]{2,1,0:T(8,128)} %mixed.1), calls=%async_computation | async-start | bytes 1048576 | tf_op jit(solution)/shard_map/all_to_all | solution.py:367
  19.4 10.5 %collective-permute-start.3 = (f32[512,128]{1,0:T(8,128)S(1)}, f32[512,128]{1,0:T(8,128)S(1)}, u32[]{:S(2)}, u32[]{:S(2)}) collective-permute-start(f32[512,128]{1,0:T(8,128)S(1)} %pad_maximum_fusion.refs_0_), channel_id=1, source_target_pairs={{0,64},{64,128},{128,192},{192,0},{16,80},{80,144},{144,208},{208,... | collective-permute-start | bytes 786440 | tf_op jit(solution)/shard_map/ppermute | solution.py:331
  20.8 9.5 %collective-permute-start.4 = (f32[512,128]{1,0:T(8,128)S(1)}, f32[512,128]{1,0:T(8,128)S(1)}, u32[]{:S(2)}, u32[]{:S(2)}) collective-permute-start(f32[512,128]{1,0:T(8,128)S(1)} %pad_maximum_fusion.refs_0_), channel_id=1, source_target_pairs={{0,192},{64,0},{128,64},{192,128},{16,208},{80,16},{144,80},{208,1... | collective-permute-start | bytes 786440 | tf_op jit(solution)/shard_map/ppermute | solution.py:331
  21.4 9.3 %collective-permute-start.5 = (f32[512,128]{1,0:T(8,128)S(1)}, f32[512,128]{1,0:T(8,128)S(1)}, u32[]{:S(2)}, u32[]{:S(2)}) collective-permute-start(f32[512,128]{1,0:T(8,128)S(1)} %pad_maximum_fusion.refs_0_), channel_id=1, source_target_pairs={{0,128},{64,192},{128,0},{192,64},{16,144},{80,208},{144,16},{208,... | collective-permute-start | bytes 786440 | tf_op jit(solution)/shard_map/ppermute | solution.py:331
  27.9 2.0 %copy-start = (f32[128,8192]{1,0:T(8,128)}, f32[128,8192]{1,0:T(8,128)S(1)}, u32[]{:S(2)}) copy-start(f32[128,8192]{1,0:T(8,128)S(1)} %get-tuple-element.21.refs_8_) | copy-start | bytes 12582916
  29.9 1.5 %collective-permute-start.6 = (f32[512,128]{1,0:T(8,128)S(1)}, f32[512,128]{1,0:T(8,128)S(1)}, u32[]{:S(2)}, u32[]{:S(2)}) collective-permute-start(f32[512,128]{1,0:T(8,128)S(1)} %pad_maximum_fusion.refs_0_), channel_id=1, source_target_pairs={{0,8},{8,0},{1,9},{9,1},{2,10},{10,2},{3,11},{11,3},{4,12},{12,4},... | collective-permute-start | bytes 786440 | tf_op jit(solution)/shard_map/ppermute | solution.py:371
  29.9 1.9 %collective-permute-start.7 = (f32[512,128]{1,0:T(8,128)S(1)}, f32[512,128]{1,0:T(8,128)S(1)}, u32[]{:S(2)}, u32[]{:S(2)}) collective-permute-start(f32[512,128]{1,0:T(8,128)S(1)} %collective-permute-done.3.refs_1_), channel_id=1, source_target_pairs={{0,8},{8,0},{1,9},{9,1},{2,10},{10,2},{3,11},{11,3},{4,12},{12,4},... | collective-permute-start | bytes 786440 | tf_op jit(solution)/shard_map/ppermute | solution.py:371
  30.4 1.8 %collective-permute-start.8 = (f32[512,128]{1,0:T(8,128)S(1)}, f32[512,128]{1,0:T(8,128)S(1)}, u32[]{:S(2)}, u32[]{:S(2)}) collective-permute-start(f32[512,128]{1,0:T(8,128)S(1)} %collective-permute-done.4.refs_2_), channel_id=1, source_target_pairs={{0,8},{8,0},{1,9},{9,1},{2,10},{10,2},{3,11},{11,3},{4,12},{12,4},... | collective-permute-start | bytes 786440 | tf_op jit(solution)/shard_map/ppermute | solution.py:371
  30.7 1.8 %collective-permute-start.9 = (f32[512,128]{1,0:T(8,128)S(1)}, f32[512,128]{1,0:T(8,128)S(1)}, u32[]{:S(2)}, u32[]{:S(2)}) collective-permute-start(f32[512,128]{1,0:T(8,128)S(1)} %collective-permute-done.5.refs_3_), channel_id=1, source_target_pairs={{0,8},{8,0},{1,9},{9,1},{2,10},{10,2},{3,11},{11,3},{4,12},{12,4},... | collective-permute-start | bytes 786440 | tf_op jit(solution)/shard_map/ppermute | solution.py:371
  34.9 2.2 %copy-start.1 = (f32[128,8192]{1,0:T(8,128)S(1)}, f32[128,8192]{1,0:T(8,128)}, u32[]{:S(2)}) copy-start(f32[128,8192]{1,0:T(8,128)} %copy-done) | copy-start | bytes 12582916
  37.1 3.6 %copy-start.3 = (f32[2,64,4096]{2,1,0:T(8,128)S(1)}, f32[2,64,4096]{2,1,0:T(8,128)}, u32[]{:S(2)}) copy-start(f32[2,64,4096]{2,1,0:T(8,128)} %param.6) | copy-start | bytes 6291460
  40.4 26.2 %collective-permute-start.13 = (f32[128,8192]{1,0:T(8,128)S(1)}, f32[128,8192]{1,0:T(8,128)S(1)}, u32[]{:S(2)}, u32[]{:S(2)}) collective-permute-start(f32[128,8192]{1,0:T(8,128)S(1)} %copy-done.1), channel_id=1, source_target_pairs={{0,8},{8,0},{1,9},{9,1},{2,10},{10,2},{3,11},{11,3},{4,12},{12,4},... | collective-permute-start | bytes 12582920 | tf_op jit(solution)/shard_map/ppermute | solution.py:378
  40.7 25.9 %collective-permute-start.12 = (f32[128,4096]{1,0:T(8,128)S(1)}, f32[128,4096]{1,0:T(8,128)S(1)}, u32[]{:S(2)}, u32[]{:S(2)}) collective-permute-start(f32[128,4096]{1,0:T(8,128)S(1)} %bitcast.27), channel_id=1, source_target_pairs={{0,8},{8,0},{1,9},{9,1},{2,10},{10,2},{3,11},{11,3},{4,12},{12,4},... | collective-permute-start | bytes 6291464 | tf_op jit(solution)/shard_map/ppermute | solution.py:378
  64.2 2.3 %collective-permute-start.10 = (f32[8,136,128]{2,1,0:T(8,128)S(1)}, f32[8,136,128]{2,1,0:T(8,128)S(1)}, u32[]{:S(2)}, u32[]{:S(2)}) collective-permute-start(f32[8,136,128]{2,1,0:T(8,128)S(1)} %all_to_all.20.h_ref), channel_id=1, source_target_pairs={{0,8},{8,0},{1,9},{9,1},{2,10},{10,2},{3,11},{11,3},{4,12},{12,4},... | collective-permute-start | bytes 1671176 | tf_op jit(solution)/shard_map/ppermute | solution.py:376
  64.3 2.3 %collective-permute-start.11 = (f32[512,128]{1,0:T(8,128)S(1)}, f32[512,128]{1,0:T(8,128)S(1)}, u32[]{:S(2)}, u32[]{:S(2)}) collective-permute-start(f32[512,128]{1,0:T(8,128)S(1)} %get-tuple-element.19), channel_id=1, source_target_pairs={{0,8},{8,0},{1,9},{9,1},{2,10},{10,2},{3,11},{11,3},{4,12},{12,4},... | collective-permute-start | bytes 786440 | tf_op jit(solution)/shard_map/ppermute | solution.py:376

commit v3 on v2

--- a/solution.py
+++ b/solution.py
@@ -136,8 +136,14 @@
 def back_kernel(kcount, ways, place_ref, *refs):
     slots = len(ways)
     rights, refs = (refs[:slots], refs[slots : 2 * slots]), refs[2 * slots :]
-    g_ref, u_ref, h_ref, send_ref, right_ref, held_ref = refs
+    signal_ref, u_ref, h_ref, send_ref, g_ref, right_ref, held_ref, sem = refs
     lanes = u_ref.shape[1]
+    steps = sem.shape[0]
+    share = g_ref.shape[1] // steps
+    waits = []
+    for step in range(steps):
+        columns = pl.ds(step * share, share)
+        waits.append(start(signal_ref.at[:, columns], g_ref.at[:, columns], sem.at[step]))
     chips = slots * slots
     width = g_ref.shape[1] // kcount
     pieces = width // lanes
@@ -164,6 +170,8 @@
 
     total = jnp.zeros((8, lanes), F32)
     for k in range(kcount):
+        if k * steps % kcount == 0:
+            waits[k * steps // kcount].wait()
         r = jnp.concatenate(
             [
                 jnp.concatenate(
@@ -194,20 +202,22 @@
 
 
 def back(place, ways, rights, others, own, u, zs, kcount):
-    rows = own.shape[0]
+    rows, states = own.shape
     body = u.shape[0] // zs
     right = (2, rights[0].shape[0] * len(rights), rights[0].shape[1])
     return pl.pallas_call(
         functools.partial(back_kernel, kcount, ways),
-        in_specs=[SCALARS, *[WHOLE for _ in (*rights, *others)], WHOLE, WHOLE],
+        in_specs=[SCALARS, *[WHOLE for _ in (*rights, *others)], ANYWHERE, WHOLE],
         out_specs=(WHOLE, WHOLE),
         out_shape=(
             jax.ShapeDtypeStruct((zs, body + 8, rows), F32),
             jax.ShapeDtypeStruct((u.shape[0] // 2, rows), F32),
         ),
         scratch_shapes=[
+            pltpu.VMEM((rows, states), F32),
             pltpu.VMEM(right, F32),
             pltpu.VMEM(u.shape, F32),
+            pltpu.SemaphoreType.DMA((4,)),
         ],
         compiler_params=pltpu.CompilerParams(vmem_limit_bytes=20 * MIB),
         name="back",
@@ -370,7 +380,7 @@
     rights[1], g_own = lax.optimization_barrier((rights[1], g_own))
     others = [swap(part) for part in rights]
 
-    h, u_sent = back(place, ways, rights, others, g_near, u, zs, kcount)
+    h, u_sent = back(place, ways, rights, others, in_hbm(g_own), u, zs, kcount)
     h, g_later = lax.optimization_barrier((h, g_near))
     h = lax.all_to_all(h, "z", split_axis=0, concat_axis=0, tiled=True)
     h_other, u_other = swap(h), swap(u_sent)

time: 104 us -> 104 us (level)
  local copies, waits for them, and re-layouts: 4.84 us -> 2.65 us
  Pallas kernels: 18.8 us -> 20.9 us
    unnamed x10, local copies, waits for them, and re-layouts: 4.18 us -> 1.99 us
    pallas_call x1, Pallas kernels: 3.26 us -> 5.26 us  [back(): pl.pallas_call(functools.partial(back_kernel, kcount, ways), in_specs=[SC...]
where the time goes in v3:
time: 104 us
  blocking collectives  53 us (51%)
  Pallas kernels  20.9 us (20%)
  starting transfers between devices  20 us (19%)
  waiting for transfers between devices  6.03 us (6%)
  local copies, waits for them, and re-layouts  2.65 us (3%)
    all_to_all x2, blocking collectives, scatter(): lax.all_to_all(value, ('x', 'y', 'c'), split_axis=0, concat_axis=0, axis_...  29.9 us
    all_to_all x1, blocking collectives, local(): h = lax.all_to_all(h, 'z', split_axis=0, concat_axis=0, tiled=True)  23.1 us
    ppermute x6, starting transfers between devices, turn(): return lax.ppermute(value, ('x', 'y', 'c'), pairs)  9.45 us
    all_to_all x1, starting transfers between devices, local(): lax.all_to_all(u, 'z', split_axis=0, concat_axis=0, tiled=True)  8.48 us
    pallas_call x1, Pallas kernels, gradients(): pl.pallas_call(functools.partial(gradients_kernel, kcount, scale), in_spe...  6.43 us
    pallas_call x1, Pallas kernels, back(): pl.pallas_call(functools.partial(back_kernel, kcount, ways), in_specs=[SC...  5.26 us
    pallas_call x1, Pallas kernels, mixed(): pl.pallas_call(mixed_kernel, in_specs=[ANYWHERE, ANYWHERE], out_specs=WHO...  4.87 us
    pallas_call x1, Pallas kernels, signal(): pl.pallas_call(signal_kernel, in_specs=[pl.BlockSpec(memory_space=pltpu.V...  4.34 us
  transfers between devices with their start and end apart: 15, of which 7 were waited for; matrix products, arithmetic and copies ran while one was open for 0% of the time, Pallas kernels for 9%

profile of v3, /device:TPU:2, one launch (start us, length us, event | category | flops | bytes accessed | tf_op | source)
XLA Modules:
  0.0 103.7 jit_solution(4582316171978317375)
XLA Ops:
  0.6 1.7 %collective-permute-start = (f32[128,128]{1,0:T(8,128)}, f32[128,128]{1,0:T(8,128)S(1)}, u32[]{:S(2)}, u32[]{:S(2)}) collective-permute-start(f32[128,128]{1,0:T(8,128)} %bitcast.33), channel_id=1, source_target_pairs={{0,16},{16,32},{32,48},{48,0},{64,80},{80,96},{96,112},{112,64},{1... | collective-permute-start | bytes 196616 | tf_op jit(solution)/shard_map/ppermute | solution.py:341
  2.3 1.7 %collective-permute-start.1 = (f32[128,128]{1,0:T(8,128)}, f32[128,128]{1,0:T(8,128)S(1)}, u32[]{:S(2)}, u32[]{:S(2)}) collective-permute-start(f32[128,128]{1,0:T(8,128)} %bitcast.34), channel_id=1, source_target_pairs={{0,48},{16,0},{32,16},{48,32},{64,112},{80,64},{96,80},{112,96},{1... | collective-permute-start | bytes 196616 | tf_op jit(solution)/shard_map/ppermute | solution.py:341
  3.9 2.0 %collective-permute-start.2 = (f32[128,128]{1,0:T(8,128)}, f32[128,128]{1,0:T(8,128)S(1)}, u32[]{:S(2)}, u32[]{:S(2)}) collective-permute-start(f32[128,128]{1,0:T(8,128)} %bitcast.35), channel_id=1, source_target_pairs={{0,32},{16,48},{32,0},{48,16},{64,96},{80,112},{96,64},{112,80},{1... | collective-permute-start | bytes 196616 | tf_op jit(solution)/shard_map/ppermute | solution.py:341
  5.9 0.0 copy-start.4
  5.9 0.0 copy-start
  5.9 4.9 %mixed.1 = f32[8,128,128]{2,1,0:T(8,128)} custom-call(f32[128,4096]{1,0:T(8,128)} %bitcast.25, f32[8,128,512]{2,1,0:T(8,128)} %left_hbm.1), custom_call_target="tpu_custom_call" | custom-call | tf_op jit(solution)/shard_map/mixed/pallas_call | solution.py:117
  10.8 0.0 collective-permute-done
  10.8 0.0 collective-permute-done.1
  10.8 0.0 collective-permute-done.2
  10.8 0.0 copy-done.4
  10.9 8.5 %all-to-all-start = ((f32[8,128,128]{2,1,0:T(8,128)}), f32[8,128,128]{2,1,0:T(8,128)S(1)}, u32[]{:S(2)}, u32[]{:S(2)}) async-start(f32[8,128,128]{2,1,0:T(8,128)} %mixed.1), calls=%async_computation | async-start | bytes 1048576 | tf_op jit(solution)/shard_map/all_to_all | solution.py:377
  19.4 1.5 %collective-permute-start.3 = (f32[512,128]{1,0:T(8,128)S(1)}, f32[512,128]{1,0:T(8,128)S(1)}, u32[]{:S(2)}, u32[]{:S(2)}) collective-permute-start(f32[512,128]{1,0:T(8,128)S(1)} %pad_maximum_fusion.refs_0_), channel_id=1, source_target_pairs={{0,64},{64,128},{128,192},{192,0},{16,80},{80,144},{144,208},{208,... | collective-permute-start | bytes 786440 | tf_op jit(solution)/shard_map/ppermute | solution.py:341
  20.8 0.5 collective-permute-start.4
  21.4 2.1 %collective-permute-start.5 = (f32[512,128]{1,0:T(8,128)S(1)}, f32[512,128]{1,0:T(8,128)S(1)}, u32[]{:S(2)}, u32[]{:S(2)}) collective-permute-start(f32[512,128]{1,0:T(8,128)S(1)} %pad_maximum_fusion.refs_0_), channel_id=1, source_target_pairs={{0,128},{64,192},{128,0},{192,64},{16,144},{80,208},{144,16},{208,... | collective-permute-start | bytes 786440 | tf_op jit(solution)/shard_map/ppermute | solution.py:341
  23.5 0.0 copy-done
  23.5 4.3 %signal.1 = (f32[128,8192]{1,0:T(8,128)}, f32[128,8192]{1,0:T(8,128)S(1)}) custom-call(s32[2,64]{1,0:T(2,128)S(1)} %copy-done, f32[32,8192]{1,0:T(8,128)} %emission_ref.1, f32[128,8192]{1,0:T(8,128)} %bitcast.29), custom_call_target="tpu_custom_call" | custom-call | tf_op jit(solution)/shard_map/signal/pallas_call | solution.py:78
  27.9 0.0 copy-start.1
  27.9 2.0 %copy-done.1 = f32[128,8192]{1,0:T(8,128)} copy-done((f32[128,8192]{1,0:T(8,128)}, f32[128,8192]{1,0:T(8,128)S(1)}, u32[]{:S(2)}) %copy-start.1) | copy-done | bytes 4194328
  29.9 0.0 collective-permute-start.6
  29.9 0.0 collective-permute-done.3.refs_1_
  29.9 0.5 collective-permute-start.7
  30.4 0.0 collective-permute-done.4.refs_2_
  30.4 0.1 collective-permute-start.8
  30.5 0.2 collective-permute-done.5.refs_3_
  30.7 0.2 collective-permute-start.9
  30.9 0.1 pad_add_fusion.place_ref
  31.0 0.4 collective-permute-done.6.refs_4_
  31.4 0.4 collective-permute-done.7.refs_5_
  31.8 0.4 collective-permute-done.8.refs_6_
  32.1 0.4 collective-permute-done.9.refs_7_
  32.5 2.4 %all-to-all-done = f32[8,128,128]{2,1,0:T(8,128)S(1)} async-done(((f32[8,128,128]{2,1,0:T(8,128)}), f32[8,128,128]{2,1,0:T(8,128)S(1)}, u32[]{:S(2)}, u32[]{:S(2)}) %all-to-all-start) | async-done | bytes 524320 | tf_op jit(solution)/shard_map/all_to_all | solution.py:377
  34.9 0.0 copy-start.2
  34.9 0.0 copy-start.3
  34.9 5.3 %back.1 = (f32[8,136,128]{2,1,0:T(8,128)S(1)}, f32[512,128]{1,0:T(8,128)S(1)}) custom-call(s32[3]{0:T(128)S(1)} %pad_add_fusion.place_ref, f32[512,128]{1,0:T(8,128)S(1)} %pad_maximum_fusion.refs_0_, f32[512,128]{1,0:T(8,128)S(1)} %collective-permute-done.3.refs_1_, f32[512,128]{1,0:T(8,128)S(1)} %collective-permute-done.4.refs_2_, ...), custom_call_target="tpu_custom_call" | custom-call | tf_op jit(solution)/shard_map/back/pallas_call | solution.py:208
  40.2 0.0 copy-done.2
  40.2 0.3 collective-permute-start.13
  40.5 0.0 copy-done.3
  40.5 0.5 collective-permute-start.12
  41.0 23.1 %all_to_all.20.h_ref = f32[8,136,128]{2,1,0:T(8,128)S(1)} all-to-all(f32[8,136,128]{2,1,0:T(8,128)S(1)} %get-tuple-element.19), channel_id=1, replica_groups=mesh['x'=4,'y'=4,'c'=2,'z'=8] {'z'}, dimensions={0} | all-to-all | bytes 1114112 | tf_op jit(solution)/shard_map/all_to_all | solution.py:385
  64.1 0.0 collective-permute-start.10
  64.1 0.5 collective-permute-start.11
  64.6 1.8 %collective-permute-done.11.uo_ref = f32[512,128]{1,0:T(8,128)S(1)} collective-permute-done((f32[512,128]{1,0:T(8,128)S(1)}, f32[512,128]{1,0:T(8,128)S(1)}, u32[]{:S(2)}, u32[]{:S(2)}) %collective-permute-start.11) | collective-permute-done | bytes 262176 | tf_op jit(solution)/shard_map/ppermute | solution.py:386
  66.4 0.0 collective-permute-done.12.refs_1_
  66.4 0.0 collective-permute-done.10.ho_ref
  66.4 0.0 collective-permute-done.13.refs_3_
  66.4 6.4 %gradients.1 = f32[16,256,128]{2,1,0:T(8,128)S(1)} custom-call(s32[3]{0:T(128)S(1)} %pad_add_fusion.place_ref, f32[8,136,128]{2,1,0:T(8,128)S(1)} %all_to_all.20.h_ref, f32[8,136,128]{2,1,0:T(8,128)S(1)} %collective-permute-done.10.ho_ref, f32[1024,128]{1,0:T(8,128)S(1)} %bitcast.24, f32[512,128]{1,0:T(8,128)S(1)} %collective-permute-done.11.uo_ref, ...), custom_call_target="tpu_custom_call" | custom-call | tf_op jit(solution)/shard_map/gradients/pallas_call | solution.py:305
  72.9 19.2 %all_to_all.21 = f32[16,256,128]{2,1,0:T(8,128)S(1)} all-to-all(f32[16,256,128]{2,1,0:T(8,128)S(1)} %gradients.1), channel_id=1, replica_groups={{0,64,128,192},{16,80,144,208},{32,96,160,224},{48,112,176,240},{8,24,4..., dimensions={0} | all-to-all | bytes 4194304 | tf_op jit(solution)/shard_map/all_to_all | solution.py:345
  92.1 0.1 reduce_sum.20
  92.3 10.7 %all_to_all.22 = f32[4,256,128]{2,1,0:T(8,128)S(1)} all-to-all(f32[4,256,128]{2,1,0:T(8,128)S(1)} %reduce_sum.20), channel_id=1, replica_groups={{0,16,32,48},{64,80,96,112},{128,144,160,176},{192,208,224,240},{8,72,1..., dimensions={0} | all-to-all | bytes 1048576 | tf_op jit(solution)/shard_map/all_to_all | solution.py:345
  103.0 0.7 fusion
  (2 shorter events, 0.0 us)
Async XLA Ops:
  0.6 10.2 %collective-permute-start = (f32[128,128]{1,0:T(8,128)}, f32[128,128]{1,0:T(8,128)S(1)}, u32[]{:S(2)}, u32[]{:S(2)}) collective-permute-start(f32[128,128]{1,0:T(8,128)} %bitcast.33), channel_id=1, source_target_pairs={{0,16},{16,32},{32,48},{48,0},{64,80},{80,96},{96,112},{112,64},{1... | collective-permute-start | bytes 196616 | tf_op jit(solution)/shard_map/ppermute | solution.py:341
  2.3 8.5 %collective-permute-start.1 = (f32[128,128]{1,0:T(8,128)}, f32[128,128]{1,0:T(8,128)S(1)}, u32[]{:S(2)}, u32[]{:S(2)}) collective-permute-start(f32[128,128]{1,0:T(8,128)} %bitcast.34), channel_id=1, source_target_pairs={{0,48},{16,0},{32,16},{48,32},{64,112},{80,64},{96,80},{112,96},{1... | collective-permute-start | bytes 196616 | tf_op jit(solution)/shard_map/ppermute | solution.py:341
  3.9 6.9 %collective-permute-start.2 = (f32[128,128]{1,0:T(8,128)}, f32[128,128]{1,0:T(8,128)S(1)}, u32[]{:S(2)}, u32[]{:S(2)}) collective-permute-start(f32[128,128]{1,0:T(8,128)} %bitcast.35), channel_id=1, source_target_pairs={{0,32},{16,48},{32,0},{48,16},{64,96},{80,112},{96,64},{112,80},{1... | collective-permute-start | bytes 196616 | tf_op jit(solution)/shard_map/ppermute | solution.py:341
  5.9 4.9 %copy-start.4 = (f32[16,2,512]{2,1,0:T(2,128)S(1)}, f32[16,2,512]{2,1,0:T(2,128)}, u32[]{:S(2)}) copy-start(f32[16,2,512]{2,1,0:T(2,128)} %param.11) | copy-start | bytes 196612
  5.9 17.6 %copy-start = (s32[2,64]{1,0:T(2,128)S(1)}, s32[2,64]{1,0:T(2,128)}, u32[]{:S(2)}) copy-start(s32[2,64]{1,0:T(2,128)} %tok_ref.1) | copy-start | bytes 1540
  10.9 24.1 %all-to-all-start = ((f32[8,128,128]{2,1,0:T(8,128)}), f32[8,128,128]{2,1,0:T(8,128)S(1)}, u32[]{:S(2)}, u32[]{:S(2)}) async-start(f32[8,128,128]{2,1,0:T(8,128)} %mixed.1), calls=%async_computation | async-start | bytes 1048576 | tf_op jit(solution)/shard_map/all_to_all | solution.py:377
  19.4 10.5 %collective-permute-start.3 = (f32[512,128]{1,0:T(8,128)S(1)}, f32[512,128]{1,0:T(8,128)S(1)}, u32[]{:S(2)}, u32[]{:S(2)}) collective-permute-start(f32[512,128]{1,0:T(8,128)S(1)} %pad_maximum_fusion.refs_0_), channel_id=1, source_target_pairs={{0,64},{64,128},{128,192},{192,0},{16,80},{80,144},{144,208},{208,... | collective-permute-start | bytes 786440 | tf_op jit(solution)/shard_map/ppermute | solution.py:341
  20.8 9.5 %collective-permute-start.4 = (f32[512,128]{1,0:T(8,128)S(1)}, f32[512,128]{1,0:T(8,128)S(1)}, u32[]{:S(2)}, u32[]{:S(2)}) collective-permute-start(f32[512,128]{1,0:T(8,128)S(1)} %pad_maximum_fusion.refs_0_), channel_id=1, source_target_pairs={{0,192},{64,0},{128,64},{192,128},{16,208},{80,16},{144,80},{208,1... | collective-permute-start | bytes 786440 | tf_op jit(solution)/shard_map/ppermute | solution.py:341
  21.4 9.3 %collective-permute-start.5 = (f32[512,128]{1,0:T(8,128)S(1)}, f32[512,128]{1,0:T(8,128)S(1)}, u32[]{:S(2)}, u32[]{:S(2)}) collective-permute-start(f32[512,128]{1,0:T(8,128)S(1)} %pad_maximum_fusion.refs_0_), channel_id=1, source_target_pairs={{0,128},{64,192},{128,0},{192,64},{16,144},{80,208},{144,16},{208,... | collective-permute-start | bytes 786440 | tf_op jit(solution)/shard_map/ppermute | solution.py:341
  27.9 2.0 %copy-start.1 = (f32[128,8192]{1,0:T(8,128)}, f32[128,8192]{1,0:T(8,128)S(1)}, u32[]{:S(2)}) copy-start(f32[128,8192]{1,0:T(8,128)S(1)} %get-tuple-element.21) | copy-start | bytes 12582916
  29.9 1.5 %collective-permute-start.6 = (f32[512,128]{1,0:T(8,128)S(1)}, f32[512,128]{1,0:T(8,128)S(1)}, u32[]{:S(2)}, u32[]{:S(2)}) collective-permute-start(f32[512,128]{1,0:T(8,128)S(1)} %pad_maximum_fusion.refs_0_), channel_id=1, source_target_pairs={{0,8},{8,0},{1,9},{9,1},{2,10},{10,2},{3,11},{11,3},{4,12},{12,4},... | collective-permute-start | bytes 786440 | tf_op jit(solution)/shard_map/ppermute | solution.py:381
  29.9 1.9 %collective-permute-start.7 = (f32[512,128]{1,0:T(8,128)S(1)}, f32[512,128]{1,0:T(8,128)S(1)}, u32[]{:S(2)}, u32[]{:S(2)}) collective-permute-start(f32[512,128]{1,0:T(8,128)S(1)} %collective-permute-done.3.refs_1_), channel_id=1, source_target_pairs={{0,8},{8,0},{1,9},{9,1},{2,10},{10,2},{3,11},{11,3},{4,12},{12,4},... | collective-permute-start | bytes 786440 | tf_op jit(solution)/shard_map/ppermute | solution.py:381
  30.4 1.8 %collective-permute-start.8 = (f32[512,128]{1,0:T(8,128)S(1)}, f32[512,128]{1,0:T(8,128)S(1)}, u32[]{:S(2)}, u32[]{:S(2)}) collective-permute-start(f32[512,128]{1,0:T(8,128)S(1)} %collective-permute-done.4.refs_2_), channel_id=1, source_target_pairs={{0,8},{8,0},{1,9},{9,1},{2,10},{10,2},{3,11},{11,3},{4,12},{12,4},... | collective-permute-start | bytes 786440 | tf_op jit(solution)/shard_map/ppermute | solution.py:381
  30.7 1.8 %collective-permute-start.9 = (f32[512,128]{1,0:T(8,128)S(1)}, f32[512,128]{1,0:T(8,128)S(1)}, u32[]{:S(2)}, u32[]{:S(2)}) collective-permute-start(f32[512,128]{1,0:T(8,128)S(1)} %collective-permute-done.5.refs_3_), channel_id=1, source_target_pairs={{0,8},{8,0},{1,9},{9,1},{2,10},{10,2},{3,11},{11,3},{4,12},{12,4},... | collective-permute-start | bytes 786440 | tf_op jit(solution)/shard_map/ppermute | solution.py:381
  34.9 5.3 %copy-start.2 = (f32[128,8192]{1,0:T(8,128)S(1)}, f32[128,8192]{1,0:T(8,128)}, u32[]{:S(2)}) copy-start(f32[128,8192]{1,0:T(8,128)} %copy-done.1) | copy-start | bytes 12582916
  34.9 5.6 %copy-start.3 = (f32[2,64,4096]{2,1,0:T(8,128)S(1)}, f32[2,64,4096]{2,1,0:T(8,128)}, u32[]{:S(2)}) copy-start(f32[2,64,4096]{2,1,0:T(8,128)} %param.6) | copy-start | bytes 6291460
  40.2 26.2 %collective-permute-start.13 = (f32[128,8192]{1,0:T(8,128)S(1)}, f32[128,8192]{1,0:T(8,128)S(1)}, u32[]{:S(2)}, u32[]{:S(2)}) collective-permute-start(f32[128,8192]{1,0:T(8,128)S(1)} %copy-done.2), channel_id=1, source_target_pairs={{0,8},{8,0},{1,9},{9,1},{2,10},{10,2},{3,11},{11,3},{4,12},{12,4},... | collective-permute-start | bytes 12582920 | tf_op jit(solution)/shard_map/ppermute | solution.py:388
  40.5 25.9 %collective-permute-start.12 = (f32[128,4096]{1,0:T(8,128)S(1)}, f32[128,4096]{1,0:T(8,128)S(1)}, u32[]{:S(2)}, u32[]{:S(2)}) collective-permute-start(f32[128,4096]{1,0:T(8,128)S(1)} %bitcast.27), channel_id=1, source_target_pairs={{0,8},{8,0},{1,9},{9,1},{2,10},{10,2},{3,11},{11,3},{4,12},{12,4},... | collective-permute-start | bytes 6291464 | tf_op jit(solution)/shard_map/ppermute | solution.py:388
  64.1 2.3 %collective-permute-start.10 = (f32[8,136,128]{2,1,0:T(8,128)S(1)}, f32[8,136,128]{2,1,0:T(8,128)S(1)}, u32[]{:S(2)}, u32[]{:S(2)}) collective-permute-start(f32[8,136,128]{2,1,0:T(8,128)S(1)} %all_to_all.20.h_ref), channel_id=1, source_target_pairs={{0,8},{8,0},{1,9},{9,1},{2,10},{10,2},{3,11},{11,3},{4,12},{12,4},... | collective-permute-start | bytes 1671176 | tf_op jit(solution)/shard_map/ppermute | solution.py:386
  64.1 2.3 %collective-permute-start.11 = (f32[512,128]{1,0:T(8,128)S(1)}, f32[512,128]{1,0:T(8,128)S(1)}, u32[]{:S(2)}, u32[]{:S(2)}) collective-permute-start(f32[512,128]{1,0:T(8,128)S(1)} %get-tuple-element.20), channel_id=1, source_target_pairs={{0,8},{8,0},{1,9},{9,1},{2,10},{10,2},{3,11},{11,3},{4,12},{12,4},... | collective-permute-start | bytes 786440 | tf_op jit(solution)/shard_map/ppermute | solution.py:386
